TPU v7x, 512 devices: a whole 4x8x8 slice. The times are simulated.
512 devices in a mesh: blk: 16 (over z_hi, x), bulk: 32 (over y, z_lo, core).
Axes of the slice: x: 4, y: 8, z: 8 (z_hi: 4, z_lo: 2; z = z_hi * 2 + z_lo), core: 2. Of those that a mesh axis runs over, the one named last changes fastest.
Arguments:
- currents: bfloat16 [512, 2, 256, 512], P(('blk', 'bulk')), may hold values from -6 to 6
- near_blocks: bfloat16 [512, 2, 2, 512, 512], P(('blk', 'bulk')), may hold values from -0.1875 to 0.1875
- near_list: int32 [512, 1], P(('blk', 'bulk')), may hold values from 0 to 7
- radiate: bfloat16 [512, 2, 512, 384], P(('blk', 'bulk')), may hold values from -0.1875 to 0.1875
- receive: bfloat16 [512, 2, 384, 512], P(('blk', 'bulk')), may hold values from -0.21875 to 0.21875
- far_list: int32 [512, 6], P(('blk', 'bulk')), may hold values from 0 to 511, as said below
- far_count: int32 [512], P(('blk', 'bulk')), may hold values from 3 to 6, as said below
- owner: int32 [512], replicated, may hold values from 0 to 511, as said below
- translation: float32 [512, 6, 2, 384], P(('blk', 'bulk')), may hold values from -3 to 3
Outputs:
- fields: bfloat16 [512, 2, 256, 512], P(('blk', 'bulk'))
Inputs may be any that keep to these rules, and one draw needn't show every extreme that they name: A permutation of the box labels that keeps every label in its own slab: owner[L] // 32 == L // 32. `far_list`: each row names 6 distinct labels of boxes held in the row's own slab by devices other than the row's own. `far_count`: the number of leading far_list entries that are used.
All inputs are finite; a program needn't handle non-finite values.
Results may differ from a plain program's by a relative error of at most 0.0051.
Values may be sent and summed in bfloat16 or wider, within the bound.
No kernel may reach another device: no remote copies, remote signals or barrier semaphores. Data moves between devices by JAX's collectives and lax.ppermute only.
A program may use at most 64 MiB of HBM per device.

v0:
```python
import jax
import jax.numpy as jnp
from jax import lax
from jax.sharding import PartitionSpec as P


def padded(array, sides, width):
    for axis, dim in sides:
        count, length = (lax.axis_size(axis), array.shape[dim])
        up = [(i, (i + 1) % count) for i in range(count - 1)]
        down = [(j, i) for i, j in up]
        last = lax.slice_in_dim(array, length - width, length, axis=dim)
        leading = lax.slice_in_dim(array, 0, width, axis=dim)
        before = lax.ppermute(last, axis, up)
        after = lax.ppermute(leading, axis, down)
        array = jnp.concatenate([before, array, after], axis=dim)
    return array


def complex_product(left, right):
    real_part = jnp.dot(left[0], right[0], preferred_element_type=jnp.float32) - jnp.dot(
        left[1], right[1], preferred_element_type=jnp.float32
    )
    imag_part = jnp.dot(left[0], right[1], preferred_element_type=jnp.float32) + jnp.dot(
        left[1], right[0], preferred_element_type=jnp.float32
    )
    return jnp.stack([real_part, imag_part])


def per_device(
    currents, near_blocks, near_list, radiate, receive, far_list, far_count, owner, translation
):
    local = currents[0]
    grid = local[None, None]
    beside_all = padded(grid, (("blk", 0), ("bulk", 1)), 1)
    flat = beside_all.reshape((9,) + local.shape)
    position_table = jnp.array([0, 1, 2, 3, 5, 6, 7, 8], jnp.int32)
    position = position_table[near_list[0, 0]]
    neighbour = lax.dynamic_index_in_dim(flat, position, 0, keepdims=False)
    patterns = complex_product(local, radiate[0]).astype(jnp.bfloat16)
    group = lax.axis_size("bulk")
    far_slots = translation.shape[1]
    sources = owner[far_list[0]] % group
    used = (jnp.arange(far_slots, dtype=jnp.int32) < far_count[0]).astype(jnp.float32)
    masked = translation[0] * used[:, None, None]
    near = complex_product(local, near_blocks[0, 0]) + complex_product(neighbour, near_blocks[0, 1])
    everything = lax.all_gather(patterns[None], "bulk", axis=0, tiled=True)
    chosen = everything[sources].astype(jnp.float32)
    real_factor = masked[:, 0][:, None, :]
    imag_factor = masked[:, 1][:, None, :]
    incoming_re = jnp.sum(real_factor * chosen[:, 0] - imag_factor * chosen[:, 1], axis=0)
    incoming_im = jnp.sum(real_factor * chosen[:, 1] + imag_factor * chosen[:, 0], axis=0)
    incoming = jnp.stack([incoming_re, incoming_im])
    far = complex_product(incoming.astype(jnp.bfloat16), receive[0])
    return (near + far).astype(jnp.bfloat16)[None]


def solution(mesh):
    return jax.shard_map(
        per_device,
        mesh=mesh,
        in_specs=(
            P(("blk", "bulk"), None, None, None),
            P(("blk", "bulk"), None, None, None, None),
            P(("blk", "bulk"), None),
            P(("blk", "bulk"), None, None, None),
            P(("blk", "bulk"), None, None, None),
            P(("blk", "bulk"), None),
            P(("blk", "bulk")),
            P(),
            P(("blk", "bulk"), None, None, None),
        ),
        out_specs=P(("blk", "bulk"), None, None, None),
        check_vma=False,
    )
```

profile of v0, /device:TPU:191, one launch (start us, length us, event | category | flops | bytes accessed | tf_op | source)
XLA Modules:
  0.0 160.2 jit_solution(6268026799802604704)
XLA Ops:
  6.5 0.0 copy-start
  6.5 0.0 copy-start.1
  6.5 0.0 copy-start.3
  6.5 0.0 all-gather.2.cloned.1.call-start
  6.5 1.5 fusion.38
  8.0 0.0 copy-start.11
  8.0 1.4 fusion.42
  9.4 1.4 fusion.8
  10.8 0.0 copy-done.1
  10.8 0.0 copy-done.3
  10.8 0.3 fusion.9
  11.1 0.0 copy-start.12
  11.1 0.0 copy-start.2
  11.1 0.8 pad_maximum_fusion.2
  11.9 0.0 all-gather.2.cloned.1.call-update
  11.9 2.5 %collective-permute-start.1 = (bf16[1,1,2,256,512]{4,3,2,1,0:T(8,128)(2,1)S(1)}, bf16[1,1,2,256,512]{4,3,2,1,0:T(8,128)(2,1)S(1)}, u32[]{:S(2)}, u32[]{:S(2)}) collective-permute-start(bf16[1,1,2,256,512]{4,3,2,1,0:T(8,128)(2,1)S(1)} %bitcast.123), channel_id=1, source_target_pairs={{32,0},{64,32},{96,64},{128,96},{160,128},{192,160},{224,192},{256... | collective-permute-start | bytes 1572872 | tf_op jit(solution)/shard_map/ppermute | solution.py:15
  14.4 7.0 %collective-permute-start = (bf16[1,1,2,256,512]{4,3,2,1,0:T(8,128)(2,1)S(1)}, bf16[1,1,2,256,512]{4,3,2,1,0:T(8,128)(2,1)}, u32[]{:S(2)}, u32[]{:S(2)}) collective-permute-start(bf16[1,1,2,256,512]{4,3,2,1,0:T(8,128)(2,1)S(1)} %bitcast.124), channel_id=1, source_target_pairs={{0,32},{32,64},{64,96},{96,128},{128,160},{160,192},{192,224},{224... | collective-permute-start | bytes 1572872 | tf_op jit(solution)/shard_map/ppermute | solution.py:14
  21.5 0.0 copy-done.11
  22.1 0.0 copy-done
  22.2 0.6 gather_fusion
  22.8 19.2 %collective-permute-done.1 = bf16[1,1,2,256,512]{4,3,2,1,0:T(8,128)(2,1)S(1)} collective-permute-done((bf16[1,1,2,256,512]{4,3,2,1,0:T(8,128)(2,1)S(1)}, bf16[1,1,2,256,512]{4,3,2,1,0:T(8,128)(2,1)S(1)}, u32[]{:S(2)}, u32[]{:S(2)}) %collective-permute-start.1) | collective-permute-done | bytes 524320 | tf_op jit(solution)/shard_map/ppermute | solution.py:15
  42.1 0.0 copy-start.6
  42.1 3.2 %collective-permute-done = bf16[1,1,2,256,512]{4,3,2,1,0:T(8,128)(2,1)} collective-permute-done((bf16[1,1,2,256,512]{4,3,2,1,0:T(8,128)(2,1)S(1)}, bf16[1,1,2,256,512]{4,3,2,1,0:T(8,128)(2,1)}, u32[]{:S(2)}, u32[]{:S(2)}) %collective-permute-start) | collective-permute-done | bytes 524320 | tf_op jit(solution)/shard_map/ppermute | solution.py:14
  45.2 2.3 %pad_maximum_fusion.1 = bf16[3,1,2,256,512]{4,3,2,1,0:T(8,128)(2,1)} fusion(bf16[1,1,2,256,512]{4,3,2,1,0:T(8,128)(2,1)S(1)} %collective-permute-done.1, bf16[1,1,2,256,512]{4,3,2,1,0:T(8,128)(2,1)S(1)} %bitcast.125, bf16[1,1,2,256,512]{4,3,2,1,0:T(8,128)(2,1)} %collective-permute-done), kind=kLoop, calls=%fused_computation.7 | loop fusion | flops 1572864 | bytes 3145728 | tf_op jit(solution)/shard_map/concatenate | solution.py:16
  47.6 6.7 %collective-permute-start.3 = (bf16[3,1,2,256,512]{4,3,2,1,0:T(8,128)(2,1)}, bf16[3,1,2,256,512]{4,3,2,1,0:T(8,128)(2,1)}, u32[]{:S(2)}, u32[]{:S(2)}) collective-permute-start(bf16[3,1,2,256,512]{4,3,2,1,0:T(8,128)(2,1)} %pad_maximum_fusion.1), channel_id=1, source_target_pairs={{1,0},{2,1},{3,2},{4,3},{5,4},{6,5},{7,6},{8,7},{9,8},{10,9},{11,1... | collective-permute-start | bytes 4718600 | tf_op jit(solution)/shard_map/ppermute | solution.py:15
  54.3 1.9 %collective-permute-start.2 = (bf16[3,1,2,256,512]{4,3,2,1,0:T(8,128)(2,1)}, bf16[3,1,2,256,512]{4,3,2,1,0:T(8,128)(2,1)}, u32[]{:S(2)}, u32[]{:S(2)}) collective-permute-start(bf16[3,1,2,256,512]{4,3,2,1,0:T(8,128)(2,1)} %pad_maximum_fusion.1), channel_id=1, source_target_pairs={{0,1},{1,2},{2,3},{3,4},{4,5},{5,6},{6,7},{7,8},{8,9},{9,10},{10,1... | collective-permute-start | bytes 4718600 | tf_op jit(solution)/shard_map/ppermute | solution.py:14
  56.9 0.0 copy-done.12
  56.9 0.6 dynamic_slice.7
  59.5 0.0 copy-done.6
  59.5 0.0 copy-done.2
  59.5 0.3 fusion.18
  59.8 0.0 copy-start.10
  59.8 0.0 copy-start.7
  59.8 0.3 fusion.4
  60.1 0.3 fusion.22
  60.4 1.1 fusion.5
  61.5 0.0 copy-done.10
  61.5 0.1 bitcast_multiply_fusion
  61.6 57.9 %collective-permute-done.3 = bf16[3,1,2,256,512]{4,3,2,1,0:T(8,128)(2,1)} collective-permute-done((bf16[3,1,2,256,512]{4,3,2,1,0:T(8,128)(2,1)}, bf16[3,1,2,256,512]{4,3,2,1,0:T(8,128)(2,1)}, u32[]{:S(2)}, u32[]{:S(2)}) %collective-permute-start.3) | collective-permute-done | bytes 1572896 | tf_op jit(solution)/shard_map/ppermute | solution.py:15
  119.5 0.0 collective-permute-done.2
  119.5 0.0 copy-done.7
  119.5 2.4 %pad_maximum_fusion = bf16[3,3,2,256,512]{4,3,2,1,0:T(8,128)(2,1)S(1)} fusion(bf16[3,1,2,256,512]{4,3,2,1,0:T(8,128)(2,1)} %collective-permute-done.3, bf16[1,1,2,256,512]{4,3,2,1,0:T(8,128)(2,1)S(1)} %copy-done.7, bf16[1,1,2,256,512]{4,3,2,1,0:T(8,128)(2,1)S(1)} %bitcast.126, bf16[1,1,2,256,512]{4,3,2,1,0:T(8,128)(2,1)} %collective-permute-done, ...), kind=kLoop, calls=%fused_computation.2 | loop fusion | flops 9437184 | bytes 9437184 | tf_op jit(solution)/shard_map/concatenate | solution.py:16
  121.9 0.3 fusion.15
  122.2 1.2 fusion.2
  123.4 0.3 fusion.13
  123.7 1.1 fusion.3
  124.8 18.5 %all-gather.2.cloned.1.call-done = bf16[32,2,256,384]{3,2,1,0:T(8,128)(2,1)} async-done(((bf16[1,2,256,384]{3,2,1,0:T(8,128)(2,1)}), bf16[32,2,256,384]{3,2,1,0:T(8,128)(2,1)}) %all-gather.2.cloned.1.call-update) | async-done | bytes 12582928 | tf_op jit(solution)/shard_map/all_gather | solution.py:47
  143.3 5.7 %gather_fusion.1 = bf16[6,2,256,384]{3,2,1,0:T(8,128)(2,1)S(1)} fusion(bf16[32,2,256,384]{3,2,1,0:T(8,128)(2,1)} %all-gather.2.cloned.1.call-done, s32[1024]{0:T(1024)S(1)} %pad_clamp_fusion), kind=kCustom, calls=%fused_computation.1 | custom fusion | bytes 4718616 | tf_op jit(solution)/shard_map/gather | solution.py:48
  149.0 0.4 convert_element_type.30
  149.4 0.0 copy-start.4
  149.4 0.7 add_reduce_fusion
  150.1 0.5 copy-done.4
  150.5 0.3 fusion.32
  150.8 0.0 copy-start.5
  150.9 0.0 copy-start.8
  150.9 0.0 copy-start.9
  150.9 0.3 fusion.36
  151.2 0.3 fusion
  151.5 0.3 fusion.1
  151.8 0.1 copy-done.5
  151.9 0.2 copy-done.8
  152.1 0.2 copy-done.9
  152.2 1.1 fusion.11
  (7 shorter events, 0.1 us)
Async XLA Ops:
  6.5 15.6 %copy-start = (s32[512]{0:T(512)S(1)}, s32[512]{0:T(512)}, u32[]{:S(2)}) copy-start(s32[512]{0:T(512)} %param.17) | copy-start | bytes 6148
  6.5 4.3 %copy-start.1 = (bf16[1,2,256,512]{3,2,1,0:T(8,128)(2,1)S(1)}, bf16[1,2,256,512]{3,2,1,0:T(8,128)(2,1)}, u32[]{:S(2)}) copy-start(bf16[1,2,256,512]{3,2,1,0:T(8,128)(2,1)} %param.10) | copy-start | bytes 1572868
  6.5 4.3 %copy-start.3 = (bf16[1,2,512,384]{3,2,1,0:T(8,128)(2,1)S(1)}, bf16[1,2,512,384]{3,2,1,0:T(8,128)(2,1)}, u32[]{:S(2)}) copy-start(bf16[1,2,512,384]{3,2,1,0:T(8,128)(2,1)} %param.13) | copy-start | bytes 2359300
  6.5 136.7 %all-gather.2.cloned.1.call-start = ((), (), s32[]{:S(2)}) async-start(), calls=%async_computation | async-start | bytes 12976128 | tf_op jit(solution)/shard_map/all_gather | solution.py:47
  8.0 13.4 %copy-start.11 = (s32[1,6]{1,0:T(1,128)S(1)}, s32[1,6]{1,0:T(1,128)}, u32[]{:S(2)}) copy-start(s32[1,6]{1,0:T(1,128)} %param.15) | copy-start | bytes 76
  11.1 45.8 %copy-start.12 = (s32[8]{0:T(128)S(1)}, s32[8]{0:T(128)}, u32[]{:S(2)}) copy-start(s32[8]{0:T(128)} %constant.31.clone) | copy-start | bytes 100
  11.1 48.4 %copy-start.2 = (bf16[1,2,2,512,512]{4,3,2,1,0:T(8,128)(2,1)S(1)}, bf16[1,2,2,512,512]{4,3,2,1,0:T(8,128)(2,1)}, u32[]{:S(2)}) copy-start(bf16[1,2,2,512,512]{4,3,2,1,0:T(8,128)(2,1)} %param.11) | copy-start | bytes 6291460
  11.9 30.1 %collective-permute-start.1 = (bf16[1,1,2,256,512]{4,3,2,1,0:T(8,128)(2,1)S(1)}, bf16[1,1,2,256,512]{4,3,2,1,0:T(8,128)(2,1)S(1)}, u32[]{:S(2)}, u32[]{:S(2)}) collective-permute-start(bf16[1,1,2,256,512]{4,3,2,1,0:T(8,128)(2,1)S(1)} %bitcast.123), channel_id=1, source_target_pairs={{32,0},{64,32},{96,64},{128,96},{160,128},{192,160},{224,192},{256... | collective-permute-start | bytes 1572872 | tf_op jit(solution)/shard_map/ppermute | solution.py:15
  14.4 30.8 %collective-permute-start = (bf16[1,1,2,256,512]{4,3,2,1,0:T(8,128)(2,1)S(1)}, bf16[1,1,2,256,512]{4,3,2,1,0:T(8,128)(2,1)}, u32[]{:S(2)}, u32[]{:S(2)}) collective-permute-start(bf16[1,1,2,256,512]{4,3,2,1,0:T(8,128)(2,1)S(1)} %bitcast.124), channel_id=1, source_target_pairs={{0,32},{32,64},{64,96},{96,128},{128,160},{160,192},{192,224},{224... | collective-permute-start | bytes 1572872 | tf_op jit(solution)/shard_map/ppermute | solution.py:14
  42.1 17.4 %copy-start.6 = (bf16[1,1,2,256,512]{4,3,2,1,0:T(8,128)(2,1)}, bf16[1,1,2,256,512]{4,3,2,1,0:T(8,128)(2,1)S(1)}, u32[]{:S(2)}) copy-start(bf16[1,1,2,256,512]{4,3,2,1,0:T(8,128)(2,1)S(1)} %collective-permute-done.1) | copy-start | bytes 1572868
  47.6 71.9 %collective-permute-start.3 = (bf16[3,1,2,256,512]{4,3,2,1,0:T(8,128)(2,1)}, bf16[3,1,2,256,512]{4,3,2,1,0:T(8,128)(2,1)}, u32[]{:S(2)}, u32[]{:S(2)}) collective-permute-start(bf16[3,1,2,256,512]{4,3,2,1,0:T(8,128)(2,1)} %pad_maximum_fusion.1), channel_id=1, source_target_pairs={{1,0},{2,1},{3,2},{4,3},{5,4},{6,5},{7,6},{8,7},{9,8},{10,9},{11,1... | collective-permute-start | bytes 4718600 | tf_op jit(solution)/shard_map/ppermute | solution.py:15
  54.3 65.2 %collective-permute-start.2 = (bf16[3,1,2,256,512]{4,3,2,1,0:T(8,128)(2,1)}, bf16[3,1,2,256,512]{4,3,2,1,0:T(8,128)(2,1)}, u32[]{:S(2)}, u32[]{:S(2)}) collective-permute-start(bf16[3,1,2,256,512]{4,3,2,1,0:T(8,128)(2,1)} %pad_maximum_fusion.1), channel_id=1, source_target_pairs={{0,1},{1,2},{2,3},{3,4},{4,5},{5,6},{6,7},{7,8},{8,9},{9,10},{10,1... | collective-permute-start | bytes 4718600 | tf_op jit(solution)/shard_map/ppermute | solution.py:14
  59.8 1.7 %copy-start.10 = (f32[1,6,2,384]{3,2,1,0:T(2,128)S(1)}, f32[1,6,2,384]{3,2,1,0:T(2,128)}, u32[]{:S(2)}) copy-start(f32[1,6,2,384]{3,2,1,0:T(2,128)} %param.18) | copy-start | bytes 55300
  59.8 59.7 %copy-start.7 = (bf16[1,1,2,256,512]{4,3,2,1,0:T(8,128)(2,1)S(1)}, bf16[1,1,2,256,512]{4,3,2,1,0:T(8,128)(2,1)}, u32[]{:S(2)}) copy-start(bf16[1,1,2,256,512]{4,3,2,1,0:T(8,128)(2,1)} %copy-done.6) | copy-start | bytes 1572868
  149.4 1.1 copy-start.4
  150.8 1.0 copy-start.5
  150.9 1.2 copy-start.8
  150.9 1.3 copy-start.9
Sparse Core Ops, SparseCore 0:
  12.1 131.1 all-gather.1
where the time goes:
time: 161 us; the launch traced here: 160 us
  waiting for transfers between devices  98.8 us (61%)
  starting transfers between devices  18.2 us (11%)
  between operations  17 us (11%)
  matrix products  10.5 us (7%)
  local copies, waits for them, and re-layouts  7.89 us (5%)
  other arithmetic  7.81 us (5%)
    ppermute x2, waiting for transfers between devices, padded(): after = lax.ppermute(leading, axis, down)  77.1 us
    all_gather x1, waiting for transfers between devices, per_device(): everything = lax.all_gather(patterns[None], 'bulk', axis=0, tiled=True)  18.5 us
    ppermute x2, starting transfers between devices, padded(): after = lax.ppermute(leading, axis, down)  9.19 us
    ppermute x2, starting transfers between devices, padded(): before = lax.ppermute(last, axis, up)  8.96 us
    gather x1, local copies, waits for them, and re-layouts, per_device(): chosen = everything[sources].astype(jnp.float32)  5.69 us
    concatenate x2, other arithmetic, padded(): array = jnp.concatenate([before, array, after], axis=dim)  4.72 us
  transfers between devices with their start and end apart: 5, of which 4 were waited for; matrix products, arithmetic and copies ran while one was open for 7% of the time, Pallas kernels for 0%

commit v1 on v0

v1 whole, which is shorter than its diff:
```python
import jax
import jax.numpy as jnp
from jax import lax
from jax.experimental import pallas as pl
from jax.experimental.pallas import tpu as pltpu
from jax.sharding import PartitionSpec as P

F32, BF16, I32 = jnp.float32, jnp.bfloat16, jnp.int32
VMEM = pl.BlockSpec(memory_space=pltpu.VMEM)
SMEM = pl.BlockSpec(memory_space=pltpu.SMEM)
ANY = pl.BlockSpec(memory_space=pl.ANY)
LOW, MIXED, SOURCE, CODE = 16, 32, 64, 72


def dot(left, right):
    return jnp.dot(left, right, preferred_element_type=F32)


def product(left_re, left_im, right):
    return (
        dot(left_re, right[0]) - dot(left_im, right[1]),
        dot(left_re, right[1]) + dot(left_im, right[0]),
    )


def params(flops, moved):
    return dict(
        compiler_params=pltpu.CompilerParams(vmem_limit_bytes=40 << 20),
        cost_estimate=pl.CostEstimate(flops=flops, bytes_accessed=moved, transcendentals=0),
    )


def split_rows(first, second):
    top = lax.broadcasted_iota(I32, first.shape, 0) < 4
    return (
        jnp.where(top, first, pltpu.roll(second, 4, 0)),
        jnp.where(top, pltpu.roll(first, 4, 0), second),
    )


def radiate_kernel(far_list, far_count, owner, near_list, currents, radiate, translation, out, table):
    group, _, width = out.shape
    real, imag = product(currents[0], currents[1], radiate)
    waves = real.shape[0]
    table[...] = jnp.zeros_like(table)
    angles = table.shape[1]
    for k in range(translation.shape[0]):
        factor = jnp.where(k < far_count[0], translation[k], 0.0)
        high = factor.astype(BF16).astype(F32)
        for base in (0, MIXED):
            table[base + 2 * k : base + 2 * k + 2, :] = high
            table[base + LOW + 2 * k : base + LOW + 2 * k + 2, :] = factor - high
        source = lax.rem(owner[far_list[0, k]], group).astype(F32)
        table[SOURCE + k : SOURCE + k + 1, :] = jnp.full((1, angles), source, F32)
    table[CODE : CODE + 1, :] = jnp.full((1, angles), near_list[0, 0].astype(F32), F32)
    tiles = angles // 8
    real = real.T.reshape(tiles, 8, waves)
    imag = imag.T.reshape(tiles, 8, waves)
    factors = table[...].T.reshape(tiles, 8, table.shape[0])
    lane = lax.broadcasted_iota(I32, factors.shape[1:], 1)
    in_mixed = (lane >= MIXED) & (lane < SOURCE)
    for pair in range(group // 2):
        a, b, c = 3 * pair, 3 * pair + 1, 3 * pair + 2
        mixed = split_rows(real[b], imag[b])
        mixed_factors = split_rows(factors[b], factors[b])
        for side, tile in ((0, a), (1, c)):
            beside = jnp.where(in_mixed, mixed_factors[side], factors[tile])
            whole = jnp.concatenate([real[tile], imag[tile], mixed[side], beside], axis=1)
            out[2 * pair + side] = whole.astype(BF16)


def translate_kernel(chunks, out, codes, values, turned, numbers, table, sem):
    group, _, width = out.shape
    waves = width // 3
    for t in range(group):
        values[t] = chunks[t, :, :width].astype(F32)
        turned[t] = pltpu.roll(values[t, :, 2 * waves :], 4, 0)
        numbers[t : t + 1, :] = chunks[t, :, width:].astype(F32)[0:1, :].astype(I32)
    codes[...] = numbers[...]
    copy = pltpu.make_async_copy(numbers, table, sem)
    copy.start()
    copy.wait()
    sign = jnp.where(lax.broadcasted_iota(I32, (8, 1), 0) < 4, -1.0, 1.0)

    def target(t, carry):
        split = chunks[t, :, width:].astype(F32)
        factor = split + pltpu.roll(split, 128 - LOW, 1)
        real = jnp.zeros((8, waves), F32)
        imag, mixed = real, real
        for k in range(6):
            source = table[t, SOURCE + k]
            fr, fi = factor[:, 2 * k : 2 * k + 1], factor[:, 2 * k + 1 : 2 * k + 2]
            mr = factor[:, MIXED + 2 * k : MIXED + 2 * k + 1]
            mi = factor[:, MIXED + 2 * k + 1 : MIXED + 2 * k + 2] * sign
            re, im = values[source, :, :waves], values[source, :, waves : 2 * waves]
            real += fr * re - fi * im
            imag += fr * im + fi * re
            mixed += mr * values[source, :, 2 * waves :] + mi * turned[source]
        out[t] = jnp.concatenate([real, imag, mixed], axis=1).astype(BF16)
        return carry

    lax.fori_loop(0, group, target, 0)


def select_kernel(place, codes, currents, across, beyond, to_sibling, to_other, sems):
    slab, spot = place[0], place[1]
    even = lax.rem(slab, 2) == 0
    group = codes.shape[0]
    sibling = jnp.where(lax.rem(spot, 2) == 0, spot + 1, spot - 1)
    other = jnp.where(lax.rem(spot, 2) == 0, spot - 1, spot + 1)
    other = jnp.clip(other, 0, group - 1)
    for n, (partner, out) in enumerate(((sibling, to_sibling), (other, to_other))):
        code = codes[partner, CODE]
        same = (code == 3) | (code == 4)
        use_across = (code > 4) == even

        @pl.when(same)
        def _(out=out, n=n):
            pltpu.make_async_copy(currents, out, sems.at[n]).start()

        @pl.when(jnp.logical_not(same) & use_across)
        def _(out=out, n=n):
            pltpu.make_async_copy(across, out, sems.at[n]).start()

        @pl.when(jnp.logical_not(same) & jnp.logical_not(use_across))
        def _(out=out, n=n):
            pltpu.make_async_copy(beyond, out, sems.at[n]).start()

    for n, out in enumerate((to_sibling, to_other)):
        pltpu.make_async_copy(currents, out, sems.at[n]).wait()


def own_kernel(currents, blocks, out):
    real, imag = product(currents[0], currents[1], blocks)
    out[0] = real
    out[1] = imag


def near_kernel(place, near_list, own, across, beyond, sibling, other, blocks, out, chosen, sem):
    slab, spot = place[0], place[1]
    code = near_list[0, 0]
    slab_even, spot_even = lax.rem(slab, 2) == 0, lax.rem(spot, 2) == 0
    straight = (code == 1) | (code == 6)
    use_across = (code > 4) == slab_even
    onward = (code == 2) | (code == 4) | (code == 7)
    use_sibling = onward == spot_even
    for source, wanted in (
        (across, straight & use_across),
        (beyond, straight & jnp.logical_not(use_across)),
        (sibling, jnp.logical_not(straight) & use_sibling),
        (other, jnp.logical_not(straight) & jnp.logical_not(use_sibling)),
    ):

        @pl.when(wanted)
        def _(source=source):
            pltpu.make_async_copy(source, chosen, sem).start()

    pltpu.make_async_copy(across, chosen, sem).wait()
    real, imag = product(chosen[0], chosen[1], blocks)
    out[0] = own[0] + real
    out[1] = own[1] + imag


def receive_kernel(incoming, receive, near, out):
    group, _, width = incoming.shape
    waves = width // 3
    reals, imags = [], []
    for pair in range(group // 2):
        first = incoming[2 * pair].astype(F32)
        second = incoming[2 * pair + 1].astype(F32)
        mixed = split_rows(first[:, 2 * waves :], second[:, 2 * waves :])
        reals += [first[:, :waves], mixed[0], second[:, :waves]]
        imags += [first[:, waves : 2 * waves], mixed[1], second[:, waves : 2 * waves]]
    left_re = jnp.concatenate(reals, axis=0).T.astype(BF16)
    left_im = jnp.concatenate(imags, axis=0).T.astype(BF16)
    real, imag = product(left_re, left_im, receive)
    out[0] = (near[0] + real).astype(BF16)
    out[1] = (near[1] + imag).astype(BF16)


def per_device(
    currents, near_blocks, near_list, radiate, receive, far_list, far_count, owner, translation
):
    local = currents[0]
    _, waves, unknowns = local.shape
    angles = radiate.shape[-1]
    slabs, group = lax.axis_size("blk"), lax.axis_size("bulk")
    place = jnp.stack([lax.axis_index("blk"), lax.axis_index("bulk")]).astype(I32)
    inner = [(i, i ^ 1) for i in range(slabs)]
    outer = [(i, j) for m in range(1, slabs - 1, 2) for i, j in ((m, m + 1), (m + 1, m))]
    side_inner = [(i, i ^ 1) for i in range(group)]
    side_outer = [(i, j) for m in range(1, group - 1, 2) for i, j in ((m, m + 1), (m + 1, m))]
    beyond = lax.ppermute(local, "blk", outer)
    chunk = 3 * waves
    payload = pl.pallas_call(
        radiate_kernel,
        out_shape=jax.ShapeDtypeStruct((group, 8, chunk + 128), BF16),
        in_specs=[SMEM] * 4 + [VMEM] * 3,
        out_specs=VMEM,
        scratch_shapes=[pltpu.VMEM((128, angles), F32)],
        name="radiate",
        **params(8 * waves * unknowns * angles, 2 << 20),
    )(far_list, far_count, owner, near_list, local, radiate[0], translation[0])
    spread = lax.all_to_all(payload, "bulk", 0, 0, tiled=True)
    across = lax.ppermute(local, "blk", inner)
    own = pl.pallas_call(
        own_kernel,
        out_shape=jax.ShapeDtypeStruct((2, waves, unknowns), F32),
        in_specs=[VMEM] * 2,
        out_specs=VMEM,
        name="near_own",
        **params(8 * waves * unknowns * unknowns, 3 << 20),
    )(local, near_blocks[0, 0])
    translated, codes = pl.pallas_call(
        translate_kernel,
        out_shape=(
            jax.ShapeDtypeStruct((group, 8, chunk), BF16),
            jax.ShapeDtypeStruct((group, 128), I32),
        ),
        in_specs=[VMEM],
        out_specs=(VMEM, VMEM),
        scratch_shapes=[
            pltpu.VMEM((group, 8, chunk), F32),
            pltpu.VMEM((group, 8, waves), F32),
            pltpu.VMEM((group, 128), I32),
            pltpu.SMEM((group, 128), I32),
            pltpu.SemaphoreType.DMA,
        ],
        name="translate",
        **params(40 << 20, 1 << 20),
    )(spread)
    incoming = lax.all_to_all(translated, "bulk", 0, 0, tiled=True)
    to_sibling, to_other = pl.pallas_call(
        select_kernel,
        out_shape=(jax.ShapeDtypeStruct(local.shape, BF16),) * 2,
        in_specs=[SMEM] * 2 + [ANY] * 3,
        out_specs=(ANY, ANY),
        scratch_shapes=[pltpu.SemaphoreType.DMA((2,))],
        name="select",
        **params(0, 2 << 20),
    )(place, codes, local, across, beyond)
    sibling = lax.ppermute(to_sibling, "bulk", side_inner)
    other = lax.ppermute(to_other, "bulk", side_outer)
    near = pl.pallas_call(
        near_kernel,
        out_shape=jax.ShapeDtypeStruct((2, waves, unknowns), F32),
        in_specs=[SMEM] * 2 + [VMEM] + [ANY] * 4 + [VMEM],
        out_specs=VMEM,
        scratch_shapes=[pltpu.VMEM(local.shape, BF16), pltpu.SemaphoreType.DMA],
        name="near_beside",
        **params(8 * waves * unknowns * unknowns, 3 << 20),
    )(place, near_list, own, across, beyond, sibling, other, near_blocks[0, 1])
    fields = pl.pallas_call(
        receive_kernel,
        out_shape=jax.ShapeDtypeStruct(local.shape, BF16),
        in_specs=[VMEM] * 3,
        out_specs=VMEM,
        name="receive",
        **params(8 * waves * unknowns * angles, 3 << 20),
    )(incoming, receive[0], near)
    return fields[None]


def solution(mesh):
    boxes = ("blk", "bulk")
    return jax.shard_map(
        per_device,
        mesh=mesh,
        in_specs=(
            P(boxes, None, None, None),
            P(boxes, None, None, None, None),
            P(boxes, None),
            P(boxes, None, None, None),
            P(boxes, None, None, None),
            P(boxes, None),
            P(boxes),
            P(),
            P(boxes, None, None, None),
        ),
        out_specs=P(boxes, None, None, None),
        check_vma=False,
    )
```

time: 161 us -> 75 us (0.47)
  the two profiles are of different devices: /device:TPU:191 before, /device:TPU:143 now
where the time goes in v1:
time: 75 us; the launch traced here: 74.4 us
  starting transfers between devices  33.6 us (45%)
  waiting for transfers between devices  19.1 us (25%)
  Pallas kernels  14.2 us (19%)
  local copies, waits for them, and re-layouts  5.91 us (8%)
  between operations  1.44 us (2%)
    ppermute x1, waiting for transfers between devices, per_device(): other = lax.ppermute(to_other, 'bulk', side_outer)  10 us
    all_to_all x1, starting transfers between devices, per_device(): spread = lax.all_to_all(payload, 'bulk', 0, 0, tiled=True)  9.83 us
    pallas_call x1, Pallas kernels, per_device(): pl.pallas_call(translate_kernel, out_shape=(jax.ShapeDtypeStruct((group,...  7.5 us
    ppermute x1, starting transfers between devices, per_device(): other = lax.ppermute(to_other, 'bulk', side_outer)  7.32 us
    all_to_all x1, waiting for transfers between devices, per_device(): spread = lax.all_to_all(payload, 'bulk', 0, 0, tiled=True)  7 us
    ppermute x1, starting transfers between devices, per_device(): beyond = lax.ppermute(local, 'blk', outer)  6.04 us
    all_to_all x1, starting transfers between devices, per_device(): incoming = lax.all_to_all(translated, 'bulk', 0, 0, tiled=True)  5.45 us
    unnamed x14, local copies, waits for them, and re-layouts  4.23 us
  transfers between devices with their start and end apart: 6, of which 3 were waited for; matrix products, arithmetic and copies ran while one was open for 2% of the time, Pallas kernels for 14%

profile of v1, /device:TPU:143, one launch (start us, length us, event | category | flops | bytes accessed | tf_op | source)
XLA Modules:
  0.0 74.4 jit_solution(16327665605040741809)
XLA Ops:
  1.3 0.0 copy-start
  1.3 1.0 %copy-done = bf16[1,2,256,512]{3,2,1,0:T(8,128)(2,1)S(1)} copy-done((bf16[1,2,256,512]{3,2,1,0:T(8,128)(2,1)S(1)}, bf16[1,2,256,512]{3,2,1,0:T(8,128)(2,1)}, u32[]{:S(2)}) %copy-start) | copy-done | bytes 524312
  2.3 0.0 copy-start.2
  2.3 1.1 %copy-done.2 = bf16[1,2,512,384]{3,2,1,0:T(8,128)(2,1)S(1)} copy-done((bf16[1,2,512,384]{3,2,1,0:T(8,128)(2,1)S(1)}, bf16[1,2,512,384]{3,2,1,0:T(8,128)(2,1)}, u32[]{:S(2)}) %copy-start.2) | copy-done | bytes 786456
  3.5 0.0 copy-start.4
  3.5 0.7 copy-done.4
  4.2 0.0 copy-start.5
  4.2 0.7 copy-done.5
  4.9 0.0 copy-start.6
  4.9 0.7 copy-done.6
  5.5 0.0 copy-start.1
  5.5 2.1 %radiate.1 = bf16[32,8,896]{2,1,0:T(8,128)(2,1)} custom-call(s32[1,6]{1,0:T(1,128)S(1)} %copy-done.6, s32[1]{0:T(128)S(6)} %copy.11.far_count, s32[512]{0:T(512)S(1)} %copy-done.5, s32[1,1]{1,0:T(1,128)S(6)} %copy.10.near_list, bf16[2,256,512]{2,1,0:T(8,128)(2,1)S(1)} %bitcast.11, bf16[2,512,384]{2,1,0:T(8,128)(2,1)S(1)} %bitcast.16, f32[6,2,384]{2,1,0:T(2,128)S(1)} %bitcast.18), custom_call_target="tpu_custom_call" | custom-call | flops 402653184 | bytes 2097152 | tf_op jit(solution)/shard_map/radiate/pallas_call | solution.py:195
  7.7 9.8 %all-to-all-start = ((bf16[32,8,896]{2,1,0:T(8,128)(2,1)}), bf16[32,8,896]{2,1,0:T(8,128)(2,1)S(1)}, u32[]{:S(2)}, u32[]{:S(2)}) async-start(bf16[32,8,896]{2,1,0:T(8,128)(2,1)} %radiate.1), calls=%async_computation | async-start | bytes 917504 | tf_op jit(solution)/shard_map/all_to_all | solution.py:204
  17.5 0.0 copy-done.1
  17.5 6.0 %collective-permute-start.1 = (bf16[2,256,512]{2,1,0:T(8,128)(2,1)S(1)}, bf16[2,256,512]{2,1,0:T(8,128)(2,1)S(1)}, u32[]{:S(2)}, u32[]{:S(2)}) collective-permute-start(bf16[2,256,512]{2,1,0:T(8,128)(2,1)S(1)} %bitcast.12), channel_id=1, source_target_pairs={{32,64},{64,32},{96,128},{128,96},{160,192},{192,160},{224,256},{2... | collective-permute-start | bytes 1572872 | tf_op jit(solution)/shard_map/ppermute | solution.py:193
  23.6 1.9 %collective-permute-start = (bf16[2,256,512]{2,1,0:T(8,128)(2,1)S(1)}, bf16[2,256,512]{2,1,0:T(8,128)(2,1)S(1)}, u32[]{:S(2)}, u32[]{:S(2)}) collective-permute-start(bf16[2,256,512]{2,1,0:T(8,128)(2,1)S(1)} %bitcast.13), channel_id=1, source_target_pairs={{0,32},{32,0},{64,96},{96,64},{128,160},{160,128},{192,224},{224,1... | collective-permute-start | bytes 1572872 | tf_op jit(solution)/shard_map/ppermute | solution.py:205
  25.5 7.0 %all-to-all-done.chunks = bf16[32,8,896]{2,1,0:T(8,128)(2,1)S(1)} async-done(((bf16[32,8,896]{2,1,0:T(8,128)(2,1)}), bf16[32,8,896]{2,1,0:T(8,128)(2,1)S(1)}, u32[]{:S(2)}, u32[]{:S(2)}) %all-to-all-start) | async-done | bytes 458784 | tf_op jit(solution)/shard_map/all_to_all | solution.py:204
  32.5 7.5 %translate.1 = (bf16[32,8,768]{2,1,0:T(8,128)(2,1)}, s32[32,128]{1,0:T(8,128)S(1)}) custom-call(bf16[32,8,896]{2,1,0:T(8,128)(2,1)S(1)} %all-to-all-done.chunks), custom_call_target="tpu_custom_call" | custom-call | flops 41943040 | bytes 1048576 | tf_op jit(solution)/shard_map/translate/pallas_call | solution.py:214
  40.0 5.5 %all-to-all-start.1 = ((bf16[32,8,768]{2,1,0:T(8,128)(2,1)}), bf16[32,8,768]{2,1,0:T(8,128)(2,1)S(1)}, u32[]{:S(2)}, u32[]{:S(2)}) async-start(bf16[32,8,768]{2,1,0:T(8,128)(2,1)} %get-tuple-element.9), calls=%async_computation.1 | async-start | bytes 786432 | tf_op jit(solution)/shard_map/all_to_all | solution.py:232
  45.5 0.1 pad_add_fusion.place
  45.6 2.1 %collective-permute-done.1.beyond = bf16[2,256,512]{2,1,0:T(8,128)(2,1)S(1)} collective-permute-done((bf16[2,256,512]{2,1,0:T(8,128)(2,1)S(1)}, bf16[2,256,512]{2,1,0:T(8,128)(2,1)S(1)}, u32[]{:S(2)}, u32[]{:S(2)}) %collective-permute-start.1) | collective-permute-done | bytes 524320 | tf_op jit(solution)/shard_map/ppermute | solution.py:193
  47.7 0.0 collective-permute-done.across
  47.7 0.9 %select.1 = (bf16[2,256,512]{2,1,0:T(8,128)(2,1)S(1)}, bf16[2,256,512]{2,1,0:T(8,128)(2,1)S(1)}) custom-call(s32[2]{0:T(128)S(1)} %pad_add_fusion.place, s32[32,128]{1,0:T(8,128)S(1)} %get-tuple-element.10.codes, bf16[2,256,512]{2,1,0:T(8,128)(2,1)S(1)} %bitcast.14, bf16[2,256,512]{2,1,0:T(8,128)(2,1)S(1)} %collective-permute-done.across, ...), custom_call_target="tpu_custom_call" | custom-call | bytes 2097152 | tf_op jit(solution)/shard_map/select/pallas_call | solution.py:233
  48.6 3.1 %collective-permute-start.2 = (bf16[2,256,512]{2,1,0:T(8,128)(2,1)S(1)}, bf16[2,256,512]{2,1,0:T(8,128)(2,1)S(1)}, u32[]{:S(2)}, u32[]{:S(2)}) collective-permute-start(bf16[2,256,512]{2,1,0:T(8,128)(2,1)S(1)} %get-tuple-element.11), channel_id=1, source_target_pairs={{0,1},{1,0},{2,3},{3,2},{4,5},{5,4},{6,7},{7,6},{8,9},{9,8},{10,11... | collective-permute-start | bytes 1572872 | tf_op jit(solution)/shard_map/ppermute | solution.py:242
  51.7 7.3 %collective-permute-start.3 = (bf16[2,256,512]{2,1,0:T(8,128)(2,1)S(1)}, bf16[2,256,512]{2,1,0:T(8,128)(2,1)S(1)}, u32[]{:S(2)}, u32[]{:S(2)}) collective-permute-start(bf16[2,256,512]{2,1,0:T(8,128)(2,1)S(1)} %get-tuple-element.12), channel_id=1, source_target_pairs={{1,2},{2,1},{3,4},{4,3},{5,6},{6,5},{7,8},{8,7},{9,10},{10,9},{11,... | collective-permute-start | bytes 1572872 | tf_op jit(solution)/shard_map/ppermute | solution.py:243
  59.0 1.7 %slice_bitcast_fusion = (bf16[2,512,512]{2,1,0:T(8,128)(2,1)S(1)}, bf16[2,512,512]{2,1,0:T(8,128)(2,1)S(1)}) fusion(bf16[1,2,2,512,512]{4,3,2,1,0:T(8,128)(2,1)} %param.10), kind=kLoop, calls=%fused_computation | loop fusion | bytes 4194304 | tf_op jit(solution)/shard_map/squeeze | solution.py:252
  60.7 0.7 near_own.1.own
  61.4 0.0 collective-permute-done.2.sibling
  61.4 10.0 %collective-permute-done.3.other = bf16[2,256,512]{2,1,0:T(8,128)(2,1)S(1)} collective-permute-done((bf16[2,256,512]{2,1,0:T(8,128)(2,1)S(1)}, bf16[2,256,512]{2,1,0:T(8,128)(2,1)S(1)}, u32[]{:S(2)}, u32[]{:S(2)}) %collective-permute-start.3) | collective-permute-done | bytes 524320 | tf_op jit(solution)/shard_map/ppermute | solution.py:243
  71.4 0.0 copy-start.3
  71.5 1.4 %near_beside.1.near = f32[2,256,512]{2,1,0:T(8,128)S(1)} custom-call(s32[2]{0:T(128)S(1)} %pad_add_fusion.place, s32[1,1]{1,0:T(1,128)S(6)} %copy.10.near_list, f32[2,256,512]{2,1,0:T(8,128)S(1)} %near_own.1.own, bf16[2,256,512]{2,1,0:T(8,128)(2,1)S(1)} %collective-permute-done.across, bf16[2,256,512]{2,1,0:T(8,128)(2,1)S(1)} %collective-permute-done.1.beyond, ...), custom_call_target="tpu_custom_call" | custom-call | flops 536870912 | bytes 3145728 | tf_op jit(solution)/shard_map/near_beside/pallas_call | solution.py:244
  72.8 0.0 all-to-all-done.1.incoming
  72.8 0.0 copy-done.3
  72.8 1.6 %receive.1 = bf16[2,256,512]{2,1,0:T(8,128)(2,1)} custom-call(bf16[32,8,768]{2,1,0:T(8,128)(2,1)S(1)} %all-to-all-done.1.incoming, bf16[2,384,512]{2,1,0:T(8,128)(2,1)S(1)} %bitcast.17, f32[2,256,512]{2,1,0:T(8,128)S(1)} %near_beside.1.near), custom_call_target="tpu_custom_call" | custom-call | flops 402653184 | bytes 3145728 | tf_op jit(solution)/shard_map/receive/pallas_call | solution.py:253
Async XLA Ops:
  1.3 1.0 %copy-start = (bf16[1,2,256,512]{3,2,1,0:T(8,128)(2,1)S(1)}, bf16[1,2,256,512]{3,2,1,0:T(8,128)(2,1)}, u32[]{:S(2)}) copy-start(bf16[1,2,256,512]{3,2,1,0:T(8,128)(2,1)} %param.9) | copy-start | bytes 1572868
  2.3 1.1 %copy-start.2 = (bf16[1,2,512,384]{3,2,1,0:T(8,128)(2,1)S(1)}, bf16[1,2,512,384]{3,2,1,0:T(8,128)(2,1)}, u32[]{:S(2)}) copy-start(bf16[1,2,512,384]{3,2,1,0:T(8,128)(2,1)} %param.12) | copy-start | bytes 2359300
  3.5 0.7 copy-start.4
  4.2 0.7 copy-start.5
  4.9 0.7 copy-start.6
  5.5 12.0 %copy-start.1 = (bf16[1,2,256,512]{3,2,1,0:T(8,128)(2,1)S(1)}, bf16[1,2,256,512]{3,2,1,0:T(8,128)(2,1)}, u32[]{:S(2)}) copy-start(bf16[1,2,256,512]{3,2,1,0:T(8,128)(2,1)} %param.9) | copy-start | bytes 1572868
  7.7 24.8 %all-to-all-start = ((bf16[32,8,896]{2,1,0:T(8,128)(2,1)}), bf16[32,8,896]{2,1,0:T(8,128)(2,1)S(1)}, u32[]{:S(2)}, u32[]{:S(2)}) async-start(bf16[32,8,896]{2,1,0:T(8,128)(2,1)} %radiate.1), calls=%async_computation | async-start | bytes 917504 | tf_op jit(solution)/shard_map/all_to_all | solution.py:204
  17.5 30.1 %collective-permute-start.1 = (bf16[2,256,512]{2,1,0:T(8,128)(2,1)S(1)}, bf16[2,256,512]{2,1,0:T(8,128)(2,1)S(1)}, u32[]{:S(2)}, u32[]{:S(2)}) collective-permute-start(bf16[2,256,512]{2,1,0:T(8,128)(2,1)S(1)} %bitcast.12), channel_id=1, source_target_pairs={{32,64},{64,32},{96,128},{128,96},{160,192},{192,160},{224,256},{2... | collective-permute-start | bytes 1572872 | tf_op jit(solution)/shard_map/ppermute | solution.py:193
  23.6 24.1 %collective-permute-start = (bf16[2,256,512]{2,1,0:T(8,128)(2,1)S(1)}, bf16[2,256,512]{2,1,0:T(8,128)(2,1)S(1)}, u32[]{:S(2)}, u32[]{:S(2)}) collective-permute-start(bf16[2,256,512]{2,1,0:T(8,128)(2,1)S(1)} %bitcast.13), channel_id=1, source_target_pairs={{0,32},{32,0},{64,96},{96,64},{128,160},{160,128},{192,224},{224,1... | collective-permute-start | bytes 1572872 | tf_op jit(solution)/shard_map/ppermute | solution.py:205
  40.0 32.8 %all-to-all-start.1 = ((bf16[32,8,768]{2,1,0:T(8,128)(2,1)}), bf16[32,8,768]{2,1,0:T(8,128)(2,1)S(1)}, u32[]{:S(2)}, u32[]{:S(2)}) async-start(bf16[32,8,768]{2,1,0:T(8,128)(2,1)} %get-tuple-element.9), calls=%async_computation.1 | async-start | bytes 786432 | tf_op jit(solution)/shard_map/all_to_all | solution.py:232
  48.6 12.8 %collective-permute-start.2 = (bf16[2,256,512]{2,1,0:T(8,128)(2,1)S(1)}, bf16[2,256,512]{2,1,0:T(8,128)(2,1)S(1)}, u32[]{:S(2)}, u32[]{:S(2)}) collective-permute-start(bf16[2,256,512]{2,1,0:T(8,128)(2,1)S(1)} %get-tuple-element.11), channel_id=1, source_target_pairs={{0,1},{1,0},{2,3},{3,2},{4,5},{5,4},{6,7},{7,6},{8,9},{9,8},{10,11... | collective-permute-start | bytes 1572872 | tf_op jit(solution)/shard_map/ppermute | solution.py:242
  51.7 19.7 %collective-permute-start.3 = (bf16[2,256,512]{2,1,0:T(8,128)(2,1)S(1)}, bf16[2,256,512]{2,1,0:T(8,128)(2,1)S(1)}, u32[]{:S(2)}, u32[]{:S(2)}) collective-permute-start(bf16[2,256,512]{2,1,0:T(8,128)(2,1)S(1)} %get-tuple-element.12), channel_id=1, source_target_pairs={{1,2},{2,1},{3,4},{4,3},{5,6},{6,5},{7,8},{8,7},{9,10},{10,9},{11,... | collective-permute-start | bytes 1572872 | tf_op jit(solution)/shard_map/ppermute | solution.py:243
  71.4 1.4 %copy-start.3 = (bf16[1,2,384,512]{3,2,1,0:T(8,128)(2,1)S(1)}, bf16[1,2,384,512]{3,2,1,0:T(8,128)(2,1)}, u32[]{:S(2)}) copy-start(bf16[1,2,384,512]{3,2,1,0:T(8,128)(2,1)} %param.13) | copy-start | bytes 2359300

commit v2 on v1

v2 whole, which is shorter than its diff:
```python
import jax
import jax.numpy as jnp
from jax import lax
from jax.experimental import pallas as pl
from jax.experimental.pallas import tpu as pltpu
from jax.sharding import PartitionSpec as P

F32, BF16, I32 = jnp.float32, jnp.bfloat16, jnp.int32
VMEM = pl.BlockSpec(memory_space=pltpu.VMEM)
SMEM = pl.BlockSpec(memory_space=pltpu.SMEM)
ANY = pl.BlockSpec(memory_space=pl.ANY)
HBM = pl.BlockSpec(memory_space=pltpu.HBM)
LOW, MIXED, SOURCE, CODE = 16, 32, 64, 72


def dot(left, right):
    return jnp.dot(left, right, preferred_element_type=F32)


def product(left_re, left_im, right):
    return (
        dot(left_re, right[0]) - dot(left_im, right[1]),
        dot(left_re, right[1]) + dot(left_im, right[0]),
    )


def params(flops, moved, limit=40 << 20):
    return dict(
        compiler_params=pltpu.CompilerParams(vmem_limit_bytes=limit),
        cost_estimate=pl.CostEstimate(flops=flops, bytes_accessed=moved, transcendentals=0),
    )


def split_rows(first, second):
    top = lax.broadcasted_iota(I32, first.shape, 0) < 4
    return (
        jnp.where(top, first, pltpu.roll(second, 4, 0)),
        jnp.where(top, pltpu.roll(first, 4, 0), second),
    )


def radiate_kernel(
    far_list_at, far_count_at, near_list_at, owner_at, currents_at, radiate_at, translation_at, out_at,
    far_list, far_count, near_list, owner, currents, radiate, translation, table, out, sems, out_sems,
):
    small = (
        (far_list_at, far_list),
        (far_count_at, far_count),
        (near_list_at, near_list),
        (owner_at, owner),
        (translation_at, translation),
    )
    large = [(currents_at.at[p], currents.at[p]) for p in range(2)]
    large += [(radiate_at.at[p], radiate.at[p]) for p in range(2)]
    copies = [
        pltpu.make_async_copy(source, target, sems.at[n])
        for n, (source, target) in enumerate((*small, *large))
    ]
    for copy in copies:
        copy.start()
    group, _, width = out.shape
    angles = table.shape[1]
    far = translation.shape[0]
    table[...] = jnp.zeros_like(table)
    for copy in copies[: len(small)]:
        copy.wait()
    for k in range(far):
        factor = jnp.where(k < far_count[0], translation[k], 0.0)
        high = factor.astype(BF16).astype(F32)
        for base in (0, MIXED):
            table[base + 2 * k : base + 2 * k + 2, :] = high
            table[base + LOW + 2 * k : base + LOW + 2 * k + 2, :] = factor - high
        source = lax.rem(owner[far_list[0, k]], group).astype(F32)
        table[SOURCE + k : SOURCE + k + 1, :] = jnp.full((1, angles), source, F32)
    table[CODE : CODE + 1, :] = jnp.full((1, angles), near_list[0, 0].astype(F32), F32)
    for copy in copies[len(small) :]:
        copy.wait()
    waves = currents.shape[1]

    def turned(part, side):
        return lax.dot_general(radiate[part], currents[side], (((0,), (1,)), ((), ())), preferred_element_type=F32)

    real = turned(0, 0) - turned(1, 1)
    imag = turned(1, 0) + turned(0, 1)
    tiles = angles // 8
    real = real.reshape(tiles, 8, waves)
    imag = imag.reshape(tiles, 8, waves)
    factors = table[...].T.reshape(tiles, 8, table.shape[0])
    lane = lax.broadcasted_iota(I32, factors.shape[1:], 1)
    in_mixed = (lane >= MIXED) & (lane < SOURCE)
    def result(step):
        part = pl.ds(group // 4 * step, group // 4)
        return pltpu.make_async_copy(out.at[part], out_at.at[part], out_sems.at[step])

    for pair in range(group // 2):
        a, b, c = 3 * pair, 3 * pair + 1, 3 * pair + 2
        mixed = split_rows(real[b], imag[b])
        mixed_factors = split_rows(factors[b], factors[b])
        for side, tile in ((0, a), (1, c)):
            beside = jnp.where(in_mixed, mixed_factors[side], factors[tile])
            whole = jnp.concatenate([real[tile], imag[tile], mixed[side], beside], axis=1)
            out[2 * pair + side] = whole.astype(BF16)
        if pair % (group // 8) == group // 8 - 1:
            result(pair // (group // 8)).start()
    for step in range(4):
        result(step).wait()


def translate_kernel(chunks, out_at, codes, out, values, turned, numbers, table, sem, sems):
    group, _, width = out.shape
    waves = width // 3
    numbers[...] = chunks[:, :, width:].astype(F32)[:, 0, :].astype(I32)
    copy = pltpu.make_async_copy(numbers, table, sem)
    copy.start()
    for t in range(group):
        values[t] = chunks[t, :, :width].astype(F32)
        turned[t] = pltpu.roll(values[t, :, 2 * waves :], 4, 0)
    codes[...] = numbers[...]
    copy.wait()
    sign = jnp.where(lax.broadcasted_iota(I32, (8, 128), 0) < 4, -1.0, 1.0)

    def target(t):
        split = chunks[t, :, width:].astype(F32)
        factor = split + pltpu.roll(split, 128 - LOW, 1)
        signed = factor * sign
        real = jnp.zeros((8, waves), F32)
        imag, mixed = real, real
        for k in range(6):
            source = table[t, SOURCE + k]
            fr, fi = factor[:, 2 * k : 2 * k + 1], factor[:, 2 * k + 1 : 2 * k + 2]
            mr = factor[:, MIXED + 2 * k : MIXED + 2 * k + 1]
            mi = signed[:, MIXED + 2 * k + 1 : MIXED + 2 * k + 2]
            re, im = values[source, :, :waves], values[source, :, waves : 2 * waves]
            real += fr * re - fi * im
            imag += fr * im + fi * re
            mixed += mr * values[source, :, 2 * waves :] + mi * turned[source]
        out[t] = jnp.concatenate([real, imag, mixed], axis=1).astype(BF16)

    def result(step):
        part = pl.ds(8 * step, 8)
        return pltpu.make_async_copy(out.at[part], out_at.at[part], sems.at[step])

    for step in range(group // 8):
        for t in range(8):
            target(8 * step + t)
        result(step).start()
    for step in range(group // 8):
        result(step).wait()


def gate_kernel(arrived, out):
    out[0] = 0


def gate(arrived, cost):
    token = pl.pallas_call(
        gate_kernel,
        out_shape=jax.ShapeDtypeStruct((1,), I32),
        in_specs=[ANY],
        out_specs=SMEM,
        name="gate",
        **params(cost, 0),
    )(arrived)
    return lax.optimization_barrier((arrived, token))[0]


def came_relayed(place):
    end = lax.rem(place[0], 4)
    return ((end == 0) | (end == 3)) & (lax.rem(place[1], 2) == 1)


def pieces(source, target, sems):
    half = source.shape[1] // 2
    return [
        pltpu.make_async_copy(
            source.at[part, pl.ds(row, half)], target.at[part, pl.ds(row, half)], sems.at[2 * part + row // half]
        )
        for part in range(2)
        for row in (0, half)
    ]


def select_kernel(place, codes, currents, across, beyond, relayed, to_other, to_sibling, sems):
    spot = place[1]
    turned = came_relayed(place)
    for n, (step, out) in enumerate(((-1, to_other), (1, to_sibling))):
        partner = jnp.where(lax.rem(spot, 2) == 0, spot + step, spot - step)
        code = codes[jnp.clip(partner, 0, codes.shape[0] - 1), CODE]
        same = (code == 3) | (code == 4)
        use_across = (code > 4) == (lax.rem(place[0], 2) == 0)
        for source, wanted in (
            (currents, same),
            (across, jnp.logical_not(same) & use_across),
            (beyond, jnp.logical_not(same | use_across | turned)),
            (relayed, jnp.logical_not(same | use_across) & turned),
        ):

            @pl.when(wanted)
            def _(source=source, out=out, n=n):
                for copy in pieces(source, out, sems.at[n]):
                    copy.start()

    for n, out in enumerate((to_other, to_sibling)):
        for copy in pieces(currents, out, sems.at[n]):
            copy.wait()


def receive_kernel(incoming, receive, currents, blocks, out):
    group, _, width = incoming.shape
    waves = width // 3
    reals, imags = [], []
    for pair in range(group // 2):
        first = incoming[2 * pair].astype(F32)
        second = incoming[2 * pair + 1].astype(F32)
        mixed = split_rows(first[:, 2 * waves :], second[:, 2 * waves :])
        reals += [first[:, :waves], mixed[0], second[:, :waves]]
        imags += [first[:, waves : 2 * waves], mixed[1], second[:, waves : 2 * waves]]
    left_re = jnp.concatenate(reals, axis=0).T.astype(BF16)
    left_im = jnp.concatenate(imags, axis=0).T.astype(BF16)
    real, imag = product(left_re, left_im, receive)
    own_re, own_im = product(currents[0], currents[1], blocks.at[0, 0])
    out[0] = own_re + real
    out[1] = own_im + imag


def near_kernel(place, near_list, partial, across, beyond, relayed, other, sibling, blocks, out_at, chosen, out, sems, out_sems):
    code = near_list[0, 0]
    straight = (code == 1) | (code == 6)
    use_across = (code > 4) == (lax.rem(place[0], 2) == 0)
    onward = (code == 2) | (code == 4) | (code == 7)
    turned = came_relayed(place)
    use_sibling = onward == (lax.rem(place[1], 2) == 0)
    for source, wanted in (
        (across, straight & use_across),
        (beyond, straight & jnp.logical_not(use_across | turned)),
        (relayed, straight & jnp.logical_not(use_across) & turned),
        (sibling, jnp.logical_not(straight) & use_sibling),
        (other, jnp.logical_not(straight) & jnp.logical_not(use_sibling)),
    ):

        @pl.when(wanted)
        def _(source=source):
            for copy in pieces(source, chosen, sems):
                copy.start()

    waits = pieces(across, chosen, sems)
    half = chosen.shape[1] // 2

    def result(part, step):
        rows = pl.ds(step * half, half)
        return pltpu.make_async_copy(out.at[part, rows], out_at.at[0, part, rows], out_sems.at[2 * part + step])

    for step in range(2):
        rows = pl.ds(step * half, half)
        for part in range(2):
            waits[2 * part + step].wait()
        real, imag = product(chosen[0, rows], chosen[1, rows], blocks.at[0, 1])
        for part, value in enumerate((real, imag)):
            out[part, rows] = (partial[part, rows] + value).astype(BF16)
            result(part, step).start()
    for step in range(2):
        for part in range(2):
            result(part, step).wait()


def per_device(
    currents, near_blocks, near_list, radiate, receive, far_list, far_count, owner, translation
):
    local = currents[0]
    _, waves, unknowns = local.shape
    angles = radiate.shape[-1]
    slabs, group = lax.axis_size("blk"), lax.axis_size("bulk")
    row = 4
    place = jnp.stack([lax.axis_index("blk"), lax.axis_index("bulk")]).astype(I32)
    inner = [(i, i ^ 1) for i in range(slabs)]
    outer = [(i, j) for m in range(1, slabs - 1, 2) for i, j in ((m, m + 1), (m + 1, m))]
    side_inner = [(i, i ^ 1) for i in range(group)]
    side_outer = [(i, j) for m in range(1, group - 1, 2) for i, j in ((m, m + 1), (m + 1, m))]
    chunk = 3 * waves
    payload = pl.pallas_call(
        radiate_kernel,
        out_shape=jax.ShapeDtypeStruct((group, 8, chunk + 128), BF16),
        in_specs=[ANY] * 7,
        out_specs=HBM,
        scratch_shapes=[
            pltpu.SMEM(far_list.shape, I32),
            pltpu.SMEM(far_count.shape, I32),
            pltpu.SMEM(near_list.shape, I32),
            pltpu.SMEM(owner.shape, I32),
            pltpu.VMEM(local.shape, BF16),
            pltpu.VMEM(radiate.shape[1:], BF16),
            pltpu.VMEM(translation.shape[1:], F32),
            pltpu.VMEM((128, angles), F32),
            pltpu.VMEM((group, 8, chunk + 128), BF16),
            pltpu.SemaphoreType.DMA((9,)),
            pltpu.SemaphoreType.DMA((4,)),
        ],
        name="radiate",
        **params(8 * waves * unknowns * angles, 2 << 20, 60 << 20),
    )(far_list, far_count, near_list, owner, local, radiate[0], translation[0])
    spread = lax.all_to_all(payload, "bulk", 0, 0, tiled=True)
    axes = ("blk", "bulk")
    direct, aside, onward = [], [], []
    for i, j in outer:
        for spot in range(group):
            if min(i, j) % row == row - 1 and spot % 2:
                turn = i - i % row if i < j else i + row - 1
                aside.append((i * group + spot, turn * group + spot))
                onward.append((turn * group + spot, j * group + spot))
            else:
                direct.append((i * group + spot, j * group + spot))
    relayed = gate(lax.ppermute(local, axes, aside), 8_000_000_000)
    beyond = lax.ppermute(local, axes, direct), lax.ppermute(relayed, axes, onward)
    across = lax.ppermute(local, "blk", inner)
    translated, codes = pl.pallas_call(
        translate_kernel,
        out_shape=(
            jax.ShapeDtypeStruct((group, 8, chunk), BF16),
            jax.ShapeDtypeStruct((group, 128), I32),
        ),
        in_specs=[VMEM],
        out_specs=(HBM, VMEM),
        scratch_shapes=[
            pltpu.VMEM((group, 8, chunk), BF16),
            pltpu.VMEM((group, 8, chunk), F32),
            pltpu.VMEM((group, 8, waves), F32),
            pltpu.VMEM((group, 128), I32),
            pltpu.SMEM((group, 128), I32),
            pltpu.SemaphoreType.DMA,
            pltpu.SemaphoreType.DMA((group // 8,)),
        ],
        name="translate",
        **params(0, 4 << 20),
    )(spread)
    incoming = lax.all_to_all(translated, "bulk", 0, 0, tiled=True)
    to_other, to_sibling = pl.pallas_call(
        select_kernel,
        out_shape=(jax.ShapeDtypeStruct(local.shape, BF16),) * 2,
        in_specs=[SMEM] * 2 + [ANY] * 4,
        out_specs=(VMEM, VMEM),
        scratch_shapes=[pltpu.SemaphoreType.DMA((2, 4))],
        name="select",
        **params(0, 2 << 20),
    )(place, codes, local, across, *beyond)
    other = lax.ppermute(to_other, "bulk", side_outer)
    sibling = lax.ppermute(to_sibling, "bulk", side_inner)
    partial = pl.pallas_call(
        receive_kernel,
        out_shape=jax.ShapeDtypeStruct((2, waves, unknowns), F32),
        in_specs=[VMEM] * 4,
        out_specs=VMEM,
        name="receive",
        **params(8 * waves * unknowns * angles, 3 << 20),
    )(incoming, receive[0], local, near_blocks)
    return pl.pallas_call(
        near_kernel,
        out_shape=jax.ShapeDtypeStruct((1, *local.shape), BF16),
        in_specs=[SMEM] * 2 + [VMEM] + [ANY] * 5 + [VMEM],
        out_specs=HBM,
        scratch_shapes=[
            pltpu.VMEM(local.shape, BF16),
            pltpu.VMEM(local.shape, BF16),
            pltpu.SemaphoreType.DMA((4,)),
            pltpu.SemaphoreType.DMA((4,)),
        ],
        name="near",
        **params(8 * waves * unknowns * unknowns, 5 << 20),
    )(place, near_list, partial, across, *beyond, other, sibling, near_blocks)


def solution(mesh):
    boxes = ("blk", "bulk")
    return jax.shard_map(
        per_device,
        mesh=mesh,
        in_specs=(
            P(boxes, None, None, None),
            P(boxes, None, None, None, None),
            P(boxes, None),
            P(boxes, None, None, None),
            P(boxes, None, None, None),
            P(boxes, None),
            P(boxes),
            P(),
            P(boxes, None, None, None),
        ),
        out_specs=P(boxes, None, None, None),
        check_vma=False,
    )
```

time: 75 us -> 70.6 us (0.941)
  the two profiles are of different devices: /device:TPU:143 before, /device:TPU:9 now
where the time goes in v2:
time: 70.6 us; the launch traced here: 70 us
  starting transfers between devices  35.3 us (50%)
  waiting for transfers between devices  16 us (23%)
  Pallas kernels  15.2 us (22%)
  local copies, waits for them, and re-layouts  1.9 us (3%)
  between operations  1.49 us (2%)
    all_to_all x1, starting transfers between devices, per_device(): spread = lax.all_to_all(payload, 'bulk', 0, 0, tiled=True)  10.5 us
    all_to_all x1, starting transfers between devices, per_device(): incoming = lax.all_to_all(translated, 'bulk', 0, 0, tiled=True)  7.73 us
    ppermute x1, starting transfers between devices, per_device(): lax.ppermute(relayed, axes, onward)  6.14 us
    ppermute x1, waiting for transfers between devices, per_device(): relayed = gate(lax.ppermute(local, axes, aside), 8000000000)  5.94 us
    ppermute x1, waiting for transfers between devices, per_device(): other = lax.ppermute(to_other, 'bulk', side_outer)  5.42 us
    all_to_all x1, waiting for transfers between devices, per_device(): incoming = lax.all_to_all(translated, 'bulk', 0, 0, tiled=True)  4.67 us
    pallas_call x1, Pallas kernels, per_device(): pl.pallas_call(translate_kernel, out_shape=(jax.ShapeDtypeStruct((group,...  4.61 us
    pallas_call x1, Pallas kernels, per_device(): pl.pallas_call(select_kernel, out_shape=(jax.ShapeDtypeStruct(local.shape...  3.29 us
  transfers between devices with their start and end apart: 8, of which 3 were waited for; matrix products, arithmetic and copies ran while one was open for 0% of the time, Pallas kernels for 13%

profile of v2, /device:TPU:9, one launch (start us, length us, event | category | flops | bytes accessed | tf_op | source)
XLA Modules:
  0.0 70.0 jit_solution(17702002471706074506)
XLA Ops:
  0.0 0.0 copy-start.1
  1.4 2.7 %radiate.1 = bf16[32,8,896]{2,1,0:T(8,128)(2,1)} custom-call(s32[1,6]{1,0:T(1,128)} %far_list_at.1, s32[1]{0:T(128)S(6)} %copy.11.far_count_at, s32[1,1]{1,0:T(1,128)S(6)} %copy.10.near_list_at.near_list, s32[512]{0:T(512)} %owner_at.1, bf16[2,256,512]{2,1,0:T(8,128)(2,1)} %bitcast.6, bf16[2,512,384]{2,1,0:T(8,128)(2,1)} %bitcast.13, f32[6,2,384]{2,1,0:T(2,128)} %bitcast.14), custom_call_target="tpu_custom_call" | custom-call | flops 402653184 | bytes 2097152 | tf_op jit(solution)/shard_map/radiate/pallas_call | solution.py:280
  4.1 0.0 copy-start
  4.1 10.5 %all-to-all-start = ((bf16[32,8,896]{2,1,0:T(8,128)(2,1)}), bf16[32,8,896]{2,1,0:T(8,128)(2,1)}, u32[]{:S(2)}, u32[]{:S(2)}) async-start(bf16[32,8,896]{2,1,0:T(8,128)(2,1)} %radiate.1), calls=%async_computation | async-start | bytes 917504 | tf_op jit(solution)/shard_map/all_to_all | solution.py:301
  14.6 0.0 copy-done.1
  14.6 1.3 %collective-permute-start.2 = (bf16[2,256,512]{2,1,0:T(8,128)(2,1)S(1)}, bf16[2,256,512]{2,1,0:T(8,128)(2,1)}, u32[]{:S(2)}, u32[]{:S(2)}) collective-permute-start(bf16[2,256,512]{2,1,0:T(8,128)(2,1)S(1)} %bitcast.7), channel_id=1, source_target_pairs={{97,1},{99,3},{101,5},{103,7},{105,9},{107,11},{109,13},{111,15},{... | collective-permute-start | bytes 1572872 | tf_op jit(solution)/shard_map/ppermute | solution.py:312
  15.9 2.8 %collective-permute-start = (bf16[2,256,512]{2,1,0:T(8,128)(2,1)S(1)}, bf16[2,256,512]{2,1,0:T(8,128)(2,1)S(1)}, u32[]{:S(2)}, u32[]{:S(2)}) collective-permute-start(bf16[2,256,512]{2,1,0:T(8,128)(2,1)S(1)} %bitcast.8), channel_id=1, source_target_pairs={{0,32},{32,0},{64,96},{96,64},{128,160},{160,128},{192,224},{224,1... | collective-permute-start | bytes 1572872 | tf_op jit(solution)/shard_map/ppermute | solution.py:314
  18.7 1.5 %collective-permute-start.1 = (bf16[2,256,512]{2,1,0:T(8,128)(2,1)S(1)}, bf16[2,256,512]{2,1,0:T(8,128)(2,1)}, u32[]{:S(2)}, u32[]{:S(2)}) collective-permute-start(bf16[2,256,512]{2,1,0:T(8,128)(2,1)S(1)} %bitcast.9), channel_id=1, source_target_pairs={{32,64},{33,65},{34,66},{35,67},{36,68},{37,69},{38,70},{39,71},{4... | collective-permute-start | bytes 1572872 | tf_op jit(solution)/shard_map/ppermute | solution.py:313
  20.2 5.9 %collective-permute-done.2 = bf16[2,256,512]{2,1,0:T(8,128)(2,1)} collective-permute-done((bf16[2,256,512]{2,1,0:T(8,128)(2,1)S(1)}, bf16[2,256,512]{2,1,0:T(8,128)(2,1)}, u32[]{:S(2)}, u32[]{:S(2)}) %collective-permute-start.2) | collective-permute-done | bytes 524320 | tf_op jit(solution)/shard_map/ppermute | solution.py:312
  26.1 6.1 %collective-permute-start.3 = (bf16[2,256,512]{2,1,0:T(8,128)(2,1)}, bf16[2,256,512]{2,1,0:T(8,128)(2,1)}, u32[]{:S(2)}, u32[]{:S(2)}) collective-permute-start(bf16[2,256,512]{2,1,0:T(8,128)(2,1)} %collective-permute-done.2), channel_id=1, source_target_pairs={{1,129},{3,131},{5,133},{7,135},{9,137},{11,139},{13,141},{15,143}... | collective-permute-start | bytes 1572872 | tf_op jit(solution)/shard_map/ppermute | solution.py:313
  32.3 0.0 all-to-all-done.chunks
  32.3 4.6 %translate.1 = (bf16[32,8,768]{2,1,0:T(8,128)(2,1)S(1)}, s32[32,128]{1,0:T(8,128)S(1)}) custom-call(bf16[32,8,896]{2,1,0:T(8,128)(2,1)} %all-to-all-done.chunks), custom_call_target="tpu_custom_call" | custom-call | bytes 4194304 | tf_op jit(solution)/shard_map/translate/pallas_call | solution.py:315
  36.9 0.0 copy-start.3
  36.9 0.8 %copy-done.3 = bf16[32,8,768]{2,1,0:T(8,128)(2,1)} copy-done((bf16[32,8,768]{2,1,0:T(8,128)(2,1)}, bf16[32,8,768]{2,1,0:T(8,128)(2,1)S(1)}, u32[]{:S(2)}) %copy-start.3) | copy-done | bytes 393240
  37.7 7.7 %all-to-all-start.1 = ((bf16[32,8,768]{2,1,0:T(8,128)(2,1)}), bf16[32,8,768]{2,1,0:T(8,128)(2,1)S(1)}, u32[]{:S(2)}, u32[]{:S(2)}) async-start(bf16[32,8,768]{2,1,0:T(8,128)(2,1)} %copy-done.3), calls=%async_computation.1 | async-start | bytes 786432 | tf_op jit(solution)/shard_map/all_to_all | solution.py:335
  45.4 0.1 pad_add_fusion.place
  45.5 0.0 copy-start.4
  45.5 0.0 collective-permute-done.across
  45.5 0.0 collective-permute-done.1.beyond
  45.5 0.0 collective-permute-done.3.relayed
  45.5 3.3 %select.1 = (bf16[2,256,512]{2,1,0:T(8,128)(2,1)}, bf16[2,256,512]{2,1,0:T(8,128)(2,1)}) custom-call(s32[2]{0:T(128)S(1)} %pad_add_fusion.place, s32[32,128]{1,0:T(8,128)S(1)} %get-tuple-element.10.codes, bf16[2,256,512]{2,1,0:T(8,128)(2,1)S(1)} %bitcast.10, bf16[2,256,512]{2,1,0:T(8,128)(2,1)S(1)} %collective-permute-done.across, ...), custom_call_target="tpu_custom_call" | custom-call | bytes 2097152 | tf_op jit(solution)/shard_map/select/pallas_call | solution.py:336
  48.8 3.0 %collective-permute-start.4 = (bf16[2,256,512]{2,1,0:T(8,128)(2,1)}, bf16[2,256,512]{2,1,0:T(8,128)(2,1)}, u32[]{:S(2)}, u32[]{:S(2)}) collective-permute-start(bf16[2,256,512]{2,1,0:T(8,128)(2,1)} %get-tuple-element.11), channel_id=1, source_target_pairs={{1,2},{2,1},{3,4},{4,3},{5,6},{6,5},{7,8},{8,7},{9,10},{10,9},{11,... | collective-permute-start | bytes 1572872 | tf_op jit(solution)/shard_map/ppermute | solution.py:345
  51.8 0.0 copy-done.4
  51.8 2.4 %collective-permute-start.5 = (bf16[2,256,512]{2,1,0:T(8,128)(2,1)}, bf16[2,256,512]{2,1,0:T(8,128)(2,1)}, u32[]{:S(2)}, u32[]{:S(2)}) collective-permute-start(bf16[2,256,512]{2,1,0:T(8,128)(2,1)} %get-tuple-element.12), channel_id=1, source_target_pairs={{0,1},{1,0},{2,3},{3,2},{4,5},{5,4},{6,7},{7,6},{8,9},{9,8},{10,11... | collective-permute-start | bytes 1572872 | tf_op jit(solution)/shard_map/ppermute | solution.py:346
  54.2 4.7 %all-to-all-done.1.incoming = bf16[32,8,768]{2,1,0:T(8,128)(2,1)S(1)} async-done(((bf16[32,8,768]{2,1,0:T(8,128)(2,1)}), bf16[32,8,768]{2,1,0:T(8,128)(2,1)S(1)}, u32[]{:S(2)}, u32[]{:S(2)}) %all-to-all-start.1) | async-done | bytes 393248 | tf_op jit(solution)/shard_map/all_to_all | solution.py:335
  58.9 0.0 copy-done
  58.9 0.0 copy-start.2
  58.9 1.1 %copy-done.2 = bf16[1,2,384,512]{3,2,1,0:T(8,128)(2,1)S(1)} copy-done((bf16[1,2,384,512]{3,2,1,0:T(8,128)(2,1)S(1)}, bf16[1,2,384,512]{3,2,1,0:T(8,128)(2,1)}, u32[]{:S(2)}) %copy-start.2) | copy-done | bytes 786456
  60.0 0.0 copy-start.5
  60.0 1.3 %receive.1.partial = f32[2,256,512]{2,1,0:T(8,128)S(1)} custom-call(bf16[32,8,768]{2,1,0:T(8,128)(2,1)S(1)} %all-to-all-done.1.incoming, bf16[2,384,512]{2,1,0:T(8,128)(2,1)S(1)} %bitcast.12, bf16[2,256,512]{2,1,0:T(8,128)(2,1)S(1)} %bitcast.11, bf16[1,2,2,512,512]{4,3,2,1,0:T(8,128)(2,1)S(1)} %copy-done), custom_call_target="tpu_custom_call" | custom-call | flops 402653184 | bytes 3145728 | tf_op jit(solution)/shard_map/receive/pallas_call | solution.py:347
  61.4 5.4 %collective-permute-done.4.other = bf16[2,256,512]{2,1,0:T(8,128)(2,1)} collective-permute-done((bf16[2,256,512]{2,1,0:T(8,128)(2,1)}, bf16[2,256,512]{2,1,0:T(8,128)(2,1)}, u32[]{:S(2)}, u32[]{:S(2)}) %collective-permute-start.4) | collective-permute-done | bytes 524320 | tf_op jit(solution)/shard_map/ppermute | solution.py:345
  66.8 0.0 collective-permute-done.5.sibling
  66.8 0.0 copy-done.5
  66.8 3.2 %near.1 = bf16[1,2,256,512]{3,2,1,0:T(8,128)(2,1)} custom-call(s32[2]{0:T(128)S(1)} %copy-done.5, s32[1,1]{1,0:T(1,128)S(6)} %copy.10.near_list_at.near_list, f32[2,256,512]{2,1,0:T(8,128)S(1)} %receive.1.partial, bf16[2,256,512]{2,1,0:T(8,128)(2,1)S(1)} %collective-permute-done.across, bf16[2,256,512]{2,1,0:T(8,128)(2,1)} %collective-permute-done.1.beyond, ...), custom_call_target="tpu_custom_call" | custom-call | flops 536870912 | bytes 5242880 | tf_op jit(solution)/shard_map/near/pallas_call | solution.py:355
Async XLA Ops:
  0.0 14.6 %copy-start.1 = (bf16[1,2,256,512]{3,2,1,0:T(8,128)(2,1)S(1)}, bf16[1,2,256,512]{3,2,1,0:T(8,128)(2,1)}, u32[]{:S(2)}) copy-start(bf16[1,2,256,512]{3,2,1,0:T(8,128)(2,1)} %param.9) | copy-start | bytes 1572868
  4.1 54.8 %copy-start = (bf16[1,2,2,512,512]{4,3,2,1,0:T(8,128)(2,1)S(1)}, bf16[1,2,2,512,512]{4,3,2,1,0:T(8,128)(2,1)}, u32[]{:S(2)}) copy-start(bf16[1,2,2,512,512]{4,3,2,1,0:T(8,128)(2,1)} %blocks.3) | copy-start | bytes 6291460
  4.1 28.2 %all-to-all-start = ((bf16[32,8,896]{2,1,0:T(8,128)(2,1)}), bf16[32,8,896]{2,1,0:T(8,128)(2,1)}, u32[]{:S(2)}, u32[]{:S(2)}) async-start(bf16[32,8,896]{2,1,0:T(8,128)(2,1)} %radiate.1), calls=%async_computation | async-start | bytes 917504 | tf_op jit(solution)/shard_map/all_to_all | solution.py:301
  14.6 11.5 %collective-permute-start.2 = (bf16[2,256,512]{2,1,0:T(8,128)(2,1)S(1)}, bf16[2,256,512]{2,1,0:T(8,128)(2,1)}, u32[]{:S(2)}, u32[]{:S(2)}) collective-permute-start(bf16[2,256,512]{2,1,0:T(8,128)(2,1)S(1)} %bitcast.7), channel_id=1, source_target_pairs={{97,1},{99,3},{101,5},{103,7},{105,9},{107,11},{109,13},{111,15},{... | collective-permute-start | bytes 1572872 | tf_op jit(solution)/shard_map/ppermute | solution.py:312
  15.9 29.6 %collective-permute-start = (bf16[2,256,512]{2,1,0:T(8,128)(2,1)S(1)}, bf16[2,256,512]{2,1,0:T(8,128)(2,1)S(1)}, u32[]{:S(2)}, u32[]{:S(2)}) collective-permute-start(bf16[2,256,512]{2,1,0:T(8,128)(2,1)S(1)} %bitcast.8), channel_id=1, source_target_pairs={{0,32},{32,0},{64,96},{96,64},{128,160},{160,128},{192,224},{224,1... | collective-permute-start | bytes 1572872 | tf_op jit(solution)/shard_map/ppermute | solution.py:314
  18.7 26.7 %collective-permute-start.1 = (bf16[2,256,512]{2,1,0:T(8,128)(2,1)S(1)}, bf16[2,256,512]{2,1,0:T(8,128)(2,1)}, u32[]{:S(2)}, u32[]{:S(2)}) collective-permute-start(bf16[2,256,512]{2,1,0:T(8,128)(2,1)S(1)} %bitcast.9), channel_id=1, source_target_pairs={{32,64},{33,65},{34,66},{35,67},{36,68},{37,69},{38,70},{39,71},{4... | collective-permute-start | bytes 1572872 | tf_op jit(solution)/shard_map/ppermute | solution.py:313
  26.1 19.4 %collective-permute-start.3 = (bf16[2,256,512]{2,1,0:T(8,128)(2,1)}, bf16[2,256,512]{2,1,0:T(8,128)(2,1)}, u32[]{:S(2)}, u32[]{:S(2)}) collective-permute-start(bf16[2,256,512]{2,1,0:T(8,128)(2,1)} %collective-permute-done.2), channel_id=1, source_target_pairs={{1,129},{3,131},{5,133},{7,135},{9,137},{11,139},{13,141},{15,143}... | collective-permute-start | bytes 1572872 | tf_op jit(solution)/shard_map/ppermute | solution.py:313
  36.9 0.8 %copy-start.3 = (bf16[32,8,768]{2,1,0:T(8,128)(2,1)}, bf16[32,8,768]{2,1,0:T(8,128)(2,1)S(1)}, u32[]{:S(2)}) copy-start(bf16[32,8,768]{2,1,0:T(8,128)(2,1)S(1)} %get-tuple-element.9) | copy-start | bytes 1179652
  37.7 21.2 %all-to-all-start.1 = ((bf16[32,8,768]{2,1,0:T(8,128)(2,1)}), bf16[32,8,768]{2,1,0:T(8,128)(2,1)S(1)}, u32[]{:S(2)}, u32[]{:S(2)}) async-start(bf16[32,8,768]{2,1,0:T(8,128)(2,1)} %copy-done.3), calls=%async_computation.1 | async-start | bytes 786432 | tf_op jit(solution)/shard_map/all_to_all | solution.py:335
  45.5 6.4 %copy-start.4 = (s32[2]{0:T(128)}, s32[2]{0:T(128)S(1)}, u32[]{:S(2)}) copy-start(s32[2]{0:T(128)S(1)} %pad_add_fusion.place) | copy-start | bytes 28
  48.8 18.0 %collective-permute-start.4 = (bf16[2,256,512]{2,1,0:T(8,128)(2,1)}, bf16[2,256,512]{2,1,0:T(8,128)(2,1)}, u32[]{:S(2)}, u32[]{:S(2)}) collective-permute-start(bf16[2,256,512]{2,1,0:T(8,128)(2,1)} %get-tuple-element.11), channel_id=1, source_target_pairs={{1,2},{2,1},{3,4},{4,3},{5,6},{6,5},{7,8},{8,7},{9,10},{10,9},{11,... | collective-permute-start | bytes 1572872 | tf_op jit(solution)/shard_map/ppermute | solution.py:345
  51.8 14.9 %collective-permute-start.5 = (bf16[2,256,512]{2,1,0:T(8,128)(2,1)}, bf16[2,256,512]{2,1,0:T(8,128)(2,1)}, u32[]{:S(2)}, u32[]{:S(2)}) collective-permute-start(bf16[2,256,512]{2,1,0:T(8,128)(2,1)} %get-tuple-element.12), channel_id=1, source_target_pairs={{0,1},{1,0},{2,3},{3,2},{4,5},{5,4},{6,7},{7,6},{8,9},{9,8},{10,11... | collective-permute-start | bytes 1572872 | tf_op jit(solution)/shard_map/ppermute | solution.py:346
  58.9 1.1 %copy-start.2 = (bf16[1,2,384,512]{3,2,1,0:T(8,128)(2,1)S(1)}, bf16[1,2,384,512]{3,2,1,0:T(8,128)(2,1)}, u32[]{:S(2)}) copy-start(bf16[1,2,384,512]{3,2,1,0:T(8,128)(2,1)} %param.13) | copy-start | bytes 2359300
  60.0 6.8 %copy-start.5 = (s32[2]{0:T(128)S(1)}, s32[2]{0:T(128)}, u32[]{:S(2)}) copy-start(s32[2]{0:T(128)} %copy-done.4) | copy-start | bytes 28

commit v3 on v2

--- a/solution.py
+++ b/solution.py
@@ -149,19 +149,19 @@
 
 
 def gate_kernel(arrived, out):
-    out[0] = 0
+    pass
 
 
 def gate(arrived, cost):
-    token = pl.pallas_call(
+    return pl.pallas_call(
         gate_kernel,
-        out_shape=jax.ShapeDtypeStruct((1,), I32),
+        out_shape=jax.ShapeDtypeStruct(arrived.shape, arrived.dtype),
         in_specs=[ANY],
-        out_specs=SMEM,
+        out_specs=ANY,
+        input_output_aliases={0: 0},
         name="gate",
         **params(cost, 0),
     )(arrived)
-    return lax.optimization_barrier((arrived, token))[0]
 
 
 def came_relayed(place):
@@ -169,21 +169,10 @@
     return ((end == 0) | (end == 3)) & (lax.rem(place[1], 2) == 1)
 
 
-def pieces(source, target, sems):
-    half = source.shape[1] // 2
-    return [
-        pltpu.make_async_copy(
-            source.at[part, pl.ds(row, half)], target.at[part, pl.ds(row, half)], sems.at[2 * part + row // half]
-        )
-        for part in range(2)
-        for row in (0, half)
-    ]
-
-
-def select_kernel(place, codes, currents, across, beyond, relayed, to_other, to_sibling, sems):
+def select_kernel(place, codes, currents, across, beyond, relayed, to_other, to_sibling):
     spot = place[1]
     turned = came_relayed(place)
-    for n, (step, out) in enumerate(((-1, to_other), (1, to_sibling))):
+    for step, out in ((-1, to_other), (1, to_sibling)):
         partner = jnp.where(lax.rem(spot, 2) == 0, spot + step, spot - step)
         code = codes[jnp.clip(partner, 0, codes.shape[0] - 1), CODE]
         same = (code == 3) | (code == 4)
@@ -196,13 +185,8 @@
         ):
 
             @pl.when(wanted)
-            def _(source=source, out=out, n=n):
-                for copy in pieces(source, out, sems.at[n]):
-                    copy.start()
-
-    for n, out in enumerate((to_other, to_sibling)):
-        for copy in pieces(currents, out, sems.at[n]):
-            copy.wait()
+            def _(source=source, out=out):
+                out[...] = source[...]
 
 
 def receive_kernel(incoming, receive, currents, blocks, out):
@@ -223,7 +207,7 @@
     out[1] = own_im + imag
 
 
-def near_kernel(place, near_list, partial, across, beyond, relayed, other, sibling, blocks, out_at, chosen, out, sems, out_sems):
+def near_kernel(place, near_list, partial, across, beyond, relayed, other, sibling, blocks, out_at, chosen, out, out_sems):
     code = near_list[0, 0]
     straight = (code == 1) | (code == 6)
     use_across = (code > 4) == (lax.rem(place[0], 2) == 0)
@@ -240,10 +224,8 @@
 
         @pl.when(wanted)
         def _(source=source):
-            for copy in pieces(source, chosen, sems):
-                copy.start()
-
-    waits = pieces(across, chosen, sems)
+            chosen[...] = source[...]
+
     half = chosen.shape[1] // 2
 
     def result(part, step):
@@ -252,8 +234,6 @@
 
     for step in range(2):
         rows = pl.ds(step * half, half)
-        for part in range(2):
-            waits[2 * part + step].wait()
         real, imag = product(chosen[0, rows], chosen[1, rows], blocks.at[0, 1])
         for part, value in enumerate((real, imag)):
             out[part, rows] = (partial[part, rows] + value).astype(BF16)
@@ -309,7 +289,7 @@
                 onward.append((turn * group + spot, j * group + spot))
             else:
                 direct.append((i * group + spot, j * group + spot))
-    relayed = gate(lax.ppermute(local, axes, aside), 8_000_000_000)
+    relayed = gate(lax.ppermute(local, axes, aside), 3_000_000_000)
     beyond = lax.ppermute(local, axes, direct), lax.ppermute(relayed, axes, onward)
     across = lax.ppermute(local, "blk", inner)
     translated, codes = pl.pallas_call(
@@ -330,15 +310,14 @@
             pltpu.SemaphoreType.DMA((group // 8,)),
         ],
         name="translate",
-        **params(0, 4 << 20),
+        **params(40 << 20, 1 << 20),
     )(spread)
     incoming = lax.all_to_all(translated, "bulk", 0, 0, tiled=True)
     to_other, to_sibling = pl.pallas_call(
         select_kernel,
         out_shape=(jax.ShapeDtypeStruct(local.shape, BF16),) * 2,
-        in_specs=[SMEM] * 2 + [ANY] * 4,
+        in_specs=[SMEM] * 2 + [VMEM] * 4,
         out_specs=(VMEM, VMEM),
-        scratch_shapes=[pltpu.SemaphoreType.DMA((2, 4))],
         name="select",
         **params(0, 2 << 20),
     )(place, codes, local, across, *beyond)
@@ -355,12 +334,11 @@
     return pl.pallas_call(
         near_kernel,
         out_shape=jax.ShapeDtypeStruct((1, *local.shape), BF16),
-        in_specs=[SMEM] * 2 + [VMEM] + [ANY] * 5 + [VMEM],
+        in_specs=[SMEM] * 2 + [VMEM] * 7,
         out_specs=HBM,
         scratch_shapes=[
             pltpu.VMEM(local.shape, BF16),
             pltpu.VMEM(local.shape, BF16),
-            pltpu.SemaphoreType.DMA((4,)),
             pltpu.SemaphoreType.DMA((4,)),
         ],
         name="near",

time: 70.6 us -> 68.3 us (0.967)
  the two profiles are of different devices: /device:TPU:9 before, /device:TPU:137 now
where the time goes in v3:
time: 68.3 us; the launch traced here: 67.7 us
  starting transfers between devices  34.3 us (50%)
  waiting for transfers between devices  15.2 us (22%)
  Pallas kernels  14 us (20%)
  local copies, waits for them, and re-layouts  2.69 us (4%)
  between operations  1.42 us (2%)
    all_to_all x1, starting transfers between devices, per_device(): spread = lax.all_to_all(payload, 'bulk', 0, 0, tiled=True)  9.32 us
    ppermute x1, starting transfers between devices, per_device(): lax.ppermute(relayed, axes, onward)  6.24 us
    all_to_all x1, waiting for transfers between devices, per_device(): incoming = lax.all_to_all(translated, 'bulk', 0, 0, tiled=True)  5.83 us
    all_to_all x1, starting transfers between devices, per_device(): incoming = lax.all_to_all(translated, 'bulk', 0, 0, tiled=True)  5.44 us
    ppermute x1, waiting for transfers between devices, per_device(): other = lax.ppermute(to_other, 'bulk', side_outer)  4.83 us
    pallas_call x1, Pallas kernels, per_device(): pl.pallas_call(translate_kernel, out_shape=(jax.ShapeDtypeStruct((group,...  4.61 us
    all_to_all x1, waiting for transfers between devices, per_device(): spread = lax.all_to_all(payload, 'bulk', 0, 0, tiled=True)  4.57 us
    ppermute x1, starting transfers between devices, per_device(): relayed = gate(lax.ppermute(local, axes, aside), 3000000000)  4.51 us
  transfers between devices with their start and end apart: 8, of which 3 were waited for; matrix products, arithmetic and copies ran while one was open for 0% of the time, Pallas kernels for 16%

profile of v3, /device:TPU:137, one launch (start us, length us, event | category | flops | bytes accessed | tf_op | source)
XLA Modules:
  0.0 67.7 jit_solution(10219839997790688544)
XLA Ops:
  0.0 0.0 copy-start.1
  0.0 4.5 %collective-permute-start.2 = (bf16[2,256,512]{2,1,0:T(8,128)(2,1)}, bf16[2,256,512]{2,1,0:T(8,128)(2,1)S(1)}, u32[]{:S(2)}, u32[]{:S(2)}) collective-permute-start(bf16[2,256,512]{2,1,0:T(8,128)(2,1)} %bitcast.6), channel_id=1, source_target_pairs={{97,1},{99,3},{101,5},{103,7},{105,9},{107,11},{109,13},{111,15},{... | collective-permute-start | bytes 1572872 | tf_op jit(solution)/shard_map/ppermute | solution.py:292
  5.8 2.7 %radiate.1 = bf16[32,8,896]{2,1,0:T(8,128)(2,1)} custom-call(s32[1,6]{1,0:T(1,128)} %far_list_at.1, s32[1]{0:T(128)S(6)} %copy.13.far_count_at, s32[1,1]{1,0:T(1,128)S(6)} %copy.12.near_list_at.near_list, s32[512]{0:T(512)} %owner_at.1, bf16[2,256,512]{2,1,0:T(8,128)(2,1)} %bitcast.7, bf16[2,512,384]{2,1,0:T(8,128)(2,1)} %bitcast.13, f32[6,2,384]{2,1,0:T(2,128)} %bitcast.14), custom_call_target="tpu_custom_call" | custom-call | flops 402653184 | bytes 2097152 | tf_op jit(solution)/shard_map/radiate/pallas_call | solution.py:260
  8.6 9.3 %all-to-all-start = ((bf16[32,8,896]{2,1,0:T(8,128)(2,1)}), bf16[32,8,896]{2,1,0:T(8,128)(2,1)}, u32[]{:S(2)}, u32[]{:S(2)}) async-start(bf16[32,8,896]{2,1,0:T(8,128)(2,1)} %radiate.1), calls=%async_computation | async-start | bytes 917504 | tf_op jit(solution)/shard_map/all_to_all | solution.py:281
  17.9 0.0 copy-done.1
  17.9 1.9 %collective-permute-start = (bf16[2,256,512]{2,1,0:T(8,128)(2,1)S(1)}, bf16[2,256,512]{2,1,0:T(8,128)(2,1)S(1)}, u32[]{:S(2)}, u32[]{:S(2)}) collective-permute-start(bf16[2,256,512]{2,1,0:T(8,128)(2,1)S(1)} %bitcast.8), channel_id=1, source_target_pairs={{0,32},{32,0},{64,96},{96,64},{128,160},{160,128},{192,224},{224,1... | collective-permute-start | bytes 1572872 | tf_op jit(solution)/shard_map/ppermute | solution.py:294
  19.8 1.5 %collective-permute-start.1 = (bf16[2,256,512]{2,1,0:T(8,128)(2,1)S(1)}, bf16[2,256,512]{2,1,0:T(8,128)(2,1)}, u32[]{:S(2)}, u32[]{:S(2)}) collective-permute-start(bf16[2,256,512]{2,1,0:T(8,128)(2,1)S(1)} %bitcast.9), channel_id=1, source_target_pairs={{32,64},{33,65},{34,66},{35,67},{36,68},{37,69},{38,70},{39,71},{4... | collective-permute-start | bytes 1572872 | tf_op jit(solution)/shard_map/ppermute | solution.py:293
  21.3 0.0 collective-permute-done.2.arrived
  21.3 0.0 copy-start.6
  21.3 0.8 %copy-done.6 = bf16[2,256,512]{2,1,0:T(8,128)(2,1)} copy-done((bf16[2,256,512]{2,1,0:T(8,128)(2,1)}, bf16[2,256,512]{2,1,0:T(8,128)(2,1)S(1)}, u32[]{:S(2)}) %copy-start.6) | copy-done | bytes 524312
  22.1 0.0 copy-start
  22.1 6.2 %collective-permute-start.3 = (bf16[2,256,512]{2,1,0:T(8,128)(2,1)}, bf16[2,256,512]{2,1,0:T(8,128)(2,1)}, u32[]{:S(2)}, u32[]{:S(2)}) collective-permute-start(bf16[2,256,512]{2,1,0:T(8,128)(2,1)} %copy-done.6), channel_id=1, source_target_pairs={{1,129},{3,131},{5,133},{7,135},{9,137},{11,139},{13,141},{15,143}... | collective-permute-start | bytes 1572872 | tf_op jit(solution)/shard_map/ppermute | solution.py:293
  28.3 4.6 %all-to-all-done.chunks = bf16[32,8,896]{2,1,0:T(8,128)(2,1)} async-done(((bf16[32,8,896]{2,1,0:T(8,128)(2,1)}), bf16[32,8,896]{2,1,0:T(8,128)(2,1)}, u32[]{:S(2)}, u32[]{:S(2)}) %all-to-all-start) | async-done | bytes 458784 | tf_op jit(solution)/shard_map/all_to_all | solution.py:281
  32.9 4.6 %translate.1 = (bf16[32,8,768]{2,1,0:T(8,128)(2,1)S(1)}, s32[32,128]{1,0:T(8,128)S(1)}) custom-call(bf16[32,8,896]{2,1,0:T(8,128)(2,1)} %all-to-all-done.chunks), custom_call_target="tpu_custom_call" | custom-call | flops 41943040 | bytes 1048576 | tf_op jit(solution)/shard_map/translate/pallas_call | solution.py:295
  37.5 0.0 copy-start.3
  37.5 0.7 %copy-done.3 = bf16[32,8,768]{2,1,0:T(8,128)(2,1)} copy-done((bf16[32,8,768]{2,1,0:T(8,128)(2,1)}, bf16[32,8,768]{2,1,0:T(8,128)(2,1)S(1)}, u32[]{:S(2)}) %copy-start.3) | copy-done | bytes 393240
  38.3 5.4 %all-to-all-start.1 = ((bf16[32,8,768]{2,1,0:T(8,128)(2,1)}), bf16[32,8,768]{2,1,0:T(8,128)(2,1)S(1)}, u32[]{:S(2)}, u32[]{:S(2)}) async-start(bf16[32,8,768]{2,1,0:T(8,128)(2,1)} %copy-done.3), calls=%async_computation.1 | async-start | bytes 786432 | tf_op jit(solution)/shard_map/all_to_all | solution.py:315
  43.7 0.1 pad_add_fusion.place
  43.8 0.0 copy-start.4
  43.8 0.0 collective-permute-done.across
  43.8 0.0 collective-permute-done.1.beyond
  43.8 0.0 collective-permute-done.3.relayed
  43.8 2.3 %select.1 = (bf16[2,256,512]{2,1,0:T(8,128)(2,1)}, bf16[2,256,512]{2,1,0:T(8,128)(2,1)}) custom-call(s32[2]{0:T(128)S(1)} %pad_add_fusion.place, s32[32,128]{1,0:T(8,128)S(1)} %get-tuple-element.10.codes, bf16[2,256,512]{2,1,0:T(8,128)(2,1)S(1)} %bitcast.10, bf16[2,256,512]{2,1,0:T(8,128)(2,1)S(1)} %collective-permute-done.across, ...), custom_call_target="tpu_custom_call" | custom-call | bytes 2097152 | tf_op jit(solution)/shard_map/select/pallas_call | solution.py:316
  46.1 3.3 %collective-permute-start.4 = (bf16[2,256,512]{2,1,0:T(8,128)(2,1)}, bf16[2,256,512]{2,1,0:T(8,128)(2,1)}, u32[]{:S(2)}, u32[]{:S(2)}) collective-permute-start(bf16[2,256,512]{2,1,0:T(8,128)(2,1)} %get-tuple-element.11), channel_id=1, source_target_pairs={{1,2},{2,1},{3,4},{4,3},{5,6},{6,5},{7,8},{8,7},{9,10},{10,9},{11,... | collective-permute-start | bytes 1572872 | tf_op jit(solution)/shard_map/ppermute | solution.py:324
  49.5 0.0 copy-done.4
  49.5 2.0 %collective-permute-start.5 = (bf16[2,256,512]{2,1,0:T(8,128)(2,1)}, bf16[2,256,512]{2,1,0:T(8,128)(2,1)}, u32[]{:S(2)}, u32[]{:S(2)}) collective-permute-start(bf16[2,256,512]{2,1,0:T(8,128)(2,1)} %get-tuple-element.12), channel_id=1, source_target_pairs={{0,1},{1,0},{2,3},{3,2},{4,5},{5,4},{6,7},{7,6},{8,9},{9,8},{10,11... | collective-permute-start | bytes 1572872 | tf_op jit(solution)/shard_map/ppermute | solution.py:325
  51.5 5.8 %all-to-all-done.1.incoming = bf16[32,8,768]{2,1,0:T(8,128)(2,1)S(1)} async-done(((bf16[32,8,768]{2,1,0:T(8,128)(2,1)}), bf16[32,8,768]{2,1,0:T(8,128)(2,1)S(1)}, u32[]{:S(2)}, u32[]{:S(2)}) %all-to-all-start.1) | async-done | bytes 393248 | tf_op jit(solution)/shard_map/all_to_all | solution.py:315
  57.4 0.0 copy-done
  57.4 0.0 copy-start.2
  57.4 1.1 %copy-done.2 = bf16[1,2,384,512]{3,2,1,0:T(8,128)(2,1)S(1)} copy-done((bf16[1,2,384,512]{3,2,1,0:T(8,128)(2,1)S(1)}, bf16[1,2,384,512]{3,2,1,0:T(8,128)(2,1)}, u32[]{:S(2)}) %copy-start.2) | copy-done | bytes 786456
  58.5 0.0 copy-start.5
  58.5 1.3 %receive.1.partial = f32[2,256,512]{2,1,0:T(8,128)S(1)} custom-call(bf16[32,8,768]{2,1,0:T(8,128)(2,1)S(1)} %all-to-all-done.1.incoming, bf16[2,384,512]{2,1,0:T(8,128)(2,1)S(1)} %bitcast.12, bf16[2,256,512]{2,1,0:T(8,128)(2,1)S(1)} %bitcast.11, bf16[1,2,2,512,512]{4,3,2,1,0:T(8,128)(2,1)S(1)} %copy-done), custom_call_target="tpu_custom_call" | custom-call | flops 402653184 | bytes 3145728 | tf_op jit(solution)/shard_map/receive/pallas_call | solution.py:326
  59.9 4.8 %collective-permute-done.4.other = bf16[2,256,512]{2,1,0:T(8,128)(2,1)} collective-permute-done((bf16[2,256,512]{2,1,0:T(8,128)(2,1)}, bf16[2,256,512]{2,1,0:T(8,128)(2,1)}, u32[]{:S(2)}, u32[]{:S(2)}) %collective-permute-start.4) | collective-permute-done | bytes 524320 | tf_op jit(solution)/shard_map/ppermute | solution.py:324
  64.7 0.0 collective-permute-done.5.sibling
  64.7 0.0 copy-done.5
  64.7 3.0 %near.1 = bf16[1,2,256,512]{3,2,1,0:T(8,128)(2,1)} custom-call(s32[2]{0:T(128)S(1)} %copy-done.5, s32[1,1]{1,0:T(1,128)S(6)} %copy.12.near_list_at.near_list, f32[2,256,512]{2,1,0:T(8,128)S(1)} %receive.1.partial, bf16[2,256,512]{2,1,0:T(8,128)(2,1)S(1)} %collective-permute-done.across, bf16[2,256,512]{2,1,0:T(8,128)(2,1)} %collective-permute-done.1.beyond, ...), custom_call_target="tpu_custom_call" | custom-call | flops 536870912 | bytes 5242880 | tf_op jit(solution)/shard_map/near/pallas_call | solution.py:334
  (1 shorter events, 0.0 us)
Async XLA Ops:
  0.0 17.9 %copy-start.1 = (bf16[1,2,256,512]{3,2,1,0:T(8,128)(2,1)S(1)}, bf16[1,2,256,512]{3,2,1,0:T(8,128)(2,1)}, u32[]{:S(2)}) copy-start(bf16[1,2,256,512]{3,2,1,0:T(8,128)(2,1)} %param.9) | copy-start | bytes 1572868
  0.0 21.3 %collective-permute-start.2 = (bf16[2,256,512]{2,1,0:T(8,128)(2,1)}, bf16[2,256,512]{2,1,0:T(8,128)(2,1)S(1)}, u32[]{:S(2)}, u32[]{:S(2)}) collective-permute-start(bf16[2,256,512]{2,1,0:T(8,128)(2,1)} %bitcast.6), channel_id=1, source_target_pairs={{97,1},{99,3},{101,5},{103,7},{105,9},{107,11},{109,13},{111,15},{... | collective-permute-start | bytes 1572872 | tf_op jit(solution)/shard_map/ppermute | solution.py:292
  8.6 24.4 %all-to-all-start = ((bf16[32,8,896]{2,1,0:T(8,128)(2,1)}), bf16[32,8,896]{2,1,0:T(8,128)(2,1)}, u32[]{:S(2)}, u32[]{:S(2)}) async-start(bf16[32,8,896]{2,1,0:T(8,128)(2,1)} %radiate.1), calls=%async_computation | async-start | bytes 917504 | tf_op jit(solution)/shard_map/all_to_all | solution.py:281
  17.9 25.9 %collective-permute-start = (bf16[2,256,512]{2,1,0:T(8,128)(2,1)S(1)}, bf16[2,256,512]{2,1,0:T(8,128)(2,1)S(1)}, u32[]{:S(2)}, u32[]{:S(2)}) collective-permute-start(bf16[2,256,512]{2,1,0:T(8,128)(2,1)S(1)} %bitcast.8), channel_id=1, source_target_pairs={{0,32},{32,0},{64,96},{96,64},{128,160},{160,128},{192,224},{224,1... | collective-permute-start | bytes 1572872 | tf_op jit(solution)/shard_map/ppermute | solution.py:294
  19.8 24.0 %collective-permute-start.1 = (bf16[2,256,512]{2,1,0:T(8,128)(2,1)S(1)}, bf16[2,256,512]{2,1,0:T(8,128)(2,1)}, u32[]{:S(2)}, u32[]{:S(2)}) collective-permute-start(bf16[2,256,512]{2,1,0:T(8,128)(2,1)S(1)} %bitcast.9), channel_id=1, source_target_pairs={{32,64},{33,65},{34,66},{35,67},{36,68},{37,69},{38,70},{39,71},{4... | collective-permute-start | bytes 1572872 | tf_op jit(solution)/shard_map/ppermute | solution.py:293
  21.3 0.8 %copy-start.6 = (bf16[2,256,512]{2,1,0:T(8,128)(2,1)}, bf16[2,256,512]{2,1,0:T(8,128)(2,1)S(1)}, u32[]{:S(2)}) copy-start(bf16[2,256,512]{2,1,0:T(8,128)(2,1)S(1)} %gate.1) | copy-start | bytes 1572868
  22.1 35.3 %copy-start = (bf16[1,2,2,512,512]{4,3,2,1,0:T(8,128)(2,1)S(1)}, bf16[1,2,2,512,512]{4,3,2,1,0:T(8,128)(2,1)}, u32[]{:S(2)}) copy-start(bf16[1,2,2,512,512]{4,3,2,1,0:T(8,128)(2,1)} %blocks.3) | copy-start | bytes 6291460
  22.1 21.7 %collective-permute-start.3 = (bf16[2,256,512]{2,1,0:T(8,128)(2,1)}, bf16[2,256,512]{2,1,0:T(8,128)(2,1)}, u32[]{:S(2)}, u32[]{:S(2)}) collective-permute-start(bf16[2,256,512]{2,1,0:T(8,128)(2,1)} %copy-done.6), channel_id=1, source_target_pairs={{1,129},{3,131},{5,133},{7,135},{9,137},{11,139},{13,141},{15,143}... | collective-permute-start | bytes 1572872 | tf_op jit(solution)/shard_map/ppermute | solution.py:293
  37.5 0.8 %copy-start.3 = (bf16[32,8,768]{2,1,0:T(8,128)(2,1)}, bf16[32,8,768]{2,1,0:T(8,128)(2,1)S(1)}, u32[]{:S(2)}) copy-start(bf16[32,8,768]{2,1,0:T(8,128)(2,1)S(1)} %get-tuple-element.9) | copy-start | bytes 1179652
  38.3 19.1 %all-to-all-start.1 = ((bf16[32,8,768]{2,1,0:T(8,128)(2,1)}), bf16[32,8,768]{2,1,0:T(8,128)(2,1)S(1)}, u32[]{:S(2)}, u32[]{:S(2)}) async-start(bf16[32,8,768]{2,1,0:T(8,128)(2,1)} %copy-done.3), calls=%async_computation.1 | async-start | bytes 786432 | tf_op jit(solution)/shard_map/all_to_all | solution.py:315
  43.8 5.7 %copy-start.4 = (s32[2]{0:T(128)}, s32[2]{0:T(128)S(1)}, u32[]{:S(2)}) copy-start(s32[2]{0:T(128)S(1)} %pad_add_fusion.place) | copy-start | bytes 28
  46.1 18.5 %collective-permute-start.4 = (bf16[2,256,512]{2,1,0:T(8,128)(2,1)}, bf16[2,256,512]{2,1,0:T(8,128)(2,1)}, u32[]{:S(2)}, u32[]{:S(2)}) collective-permute-start(bf16[2,256,512]{2,1,0:T(8,128)(2,1)} %get-tuple-element.11), channel_id=1, source_target_pairs={{1,2},{2,1},{3,4},{4,3},{5,6},{6,5},{7,8},{8,7},{9,10},{10,9},{11,... | collective-permute-start | bytes 1572872 | tf_op jit(solution)/shard_map/ppermute | solution.py:324
  49.5 15.2 %collective-permute-start.5 = (bf16[2,256,512]{2,1,0:T(8,128)(2,1)}, bf16[2,256,512]{2,1,0:T(8,128)(2,1)}, u32[]{:S(2)}, u32[]{:S(2)}) collective-permute-start(bf16[2,256,512]{2,1,0:T(8,128)(2,1)} %get-tuple-element.12), channel_id=1, source_target_pairs={{0,1},{1,0},{2,3},{3,2},{4,5},{5,4},{6,7},{7,6},{8,9},{9,8},{10,11... | collective-permute-start | bytes 1572872 | tf_op jit(solution)/shard_map/ppermute | solution.py:325
  57.4 1.1 %copy-start.2 = (bf16[1,2,384,512]{3,2,1,0:T(8,128)(2,1)S(1)}, bf16[1,2,384,512]{3,2,1,0:T(8,128)(2,1)}, u32[]{:S(2)}) copy-start(bf16[1,2,384,512]{3,2,1,0:T(8,128)(2,1)} %param.13) | copy-start | bytes 2359300
  58.5 6.2 %copy-start.5 = (s32[2]{0:T(128)S(1)}, s32[2]{0:T(128)}, u32[]{:S(2)}) copy-start(s32[2]{0:T(128)} %copy-done.4) | copy-start | bytes 28

commit v4 on v3

--- a/solution.py
+++ b/solution.py
@@ -106,15 +106,22 @@
         result(step).wait()
 
 
-def translate_kernel(chunks, out_at, codes, out, values, turned, numbers, table, sem, sems):
+def translate_kernel(chunks_at, out, codes, chunks, values, turned, numbers, table, sem, sems):
     group, _, width = out.shape
     waves = width // 3
-    numbers[...] = chunks[:, :, width:].astype(F32)[:, 0, :].astype(I32)
+    arrivals = []
+    for step in range(group // 8):
+        part = pl.ds(8 * step, 8)
+        arrivals.append(pltpu.make_async_copy(chunks_at.at[part], chunks.at[part], sems.at[step]))
+        arrivals[-1].start()
+    for step, arrival in enumerate(arrivals):
+        arrival.wait()
+        for t in range(8 * step, 8 * step + 8):
+            numbers[t : t + 1, :] = chunks[t, :, width:].astype(F32)[0:1, :].astype(I32)
+            values[t] = chunks[t, :, :width].astype(F32)
+            turned[t] = pltpu.roll(values[t, :, 2 * waves :], 4, 0)
     copy = pltpu.make_async_copy(numbers, table, sem)
     copy.start()
-    for t in range(group):
-        values[t] = chunks[t, :, :width].astype(F32)
-        turned[t] = pltpu.roll(values[t, :, 2 * waves :], 4, 0)
     codes[...] = numbers[...]
     copy.wait()
     sign = jnp.where(lax.broadcasted_iota(I32, (8, 128), 0) < 4, -1.0, 1.0)
@@ -136,16 +143,9 @@
             mixed += mr * values[source, :, 2 * waves :] + mi * turned[source]
         out[t] = jnp.concatenate([real, imag, mixed], axis=1).astype(BF16)
 
-    def result(step):
-        part = pl.ds(8 * step, 8)
-        return pltpu.make_async_copy(out.at[part], out_at.at[part], sems.at[step])
-
     for step in range(group // 8):
         for t in range(8):
             target(8 * step + t)
-        result(step).start()
-    for step in range(group // 8):
-        result(step).wait()
 
 
 def gate_kernel(arrived, out):
@@ -189,7 +189,19 @@
                 out[...] = source[...]
 
 
-def receive_kernel(incoming, receive, currents, blocks, out):
+def receive_kernel(place, near_list, incoming, receive, currents, blocks, across, beyond, relayed, out, mine):
+    use_across = (near_list[0, 0] > 4) == (lax.rem(place[0], 2) == 0)
+    turned = came_relayed(place)
+    for source, wanted in (
+        (across, use_across),
+        (beyond, jnp.logical_not(use_across | turned)),
+        (relayed, jnp.logical_not(use_across) & turned),
+    ):
+
+        @pl.when(wanted)
+        def _(source=source):
+            mine[...] = source[...]
+
     group, _, width = incoming.shape
     waves = width // 3
     reals, imags = [], []
@@ -207,17 +219,13 @@
     out[1] = own_im + imag
 
 
-def near_kernel(place, near_list, partial, across, beyond, relayed, other, sibling, blocks, out_at, chosen, out, out_sems):
+def near_kernel(place, near_list, partial, mine, other, sibling, blocks, out_at, chosen, out, out_sems):
     code = near_list[0, 0]
     straight = (code == 1) | (code == 6)
-    use_across = (code > 4) == (lax.rem(place[0], 2) == 0)
     onward = (code == 2) | (code == 4) | (code == 7)
-    turned = came_relayed(place)
     use_sibling = onward == (lax.rem(place[1], 2) == 0)
     for source, wanted in (
-        (across, straight & use_across),
-        (beyond, straight & jnp.logical_not(use_across | turned)),
-        (relayed, straight & jnp.logical_not(use_across) & turned),
+        (mine, straight),
         (sibling, jnp.logical_not(straight) & use_sibling),
         (other, jnp.logical_not(straight) & jnp.logical_not(use_sibling)),
     ):
@@ -298,10 +306,10 @@
             jax.ShapeDtypeStruct((group, 8, chunk), BF16),
             jax.ShapeDtypeStruct((group, 128), I32),
         ),
-        in_specs=[VMEM],
-        out_specs=(HBM, VMEM),
+        in_specs=[ANY],
+        out_specs=(VMEM, VMEM),
         scratch_shapes=[
-            pltpu.VMEM((group, 8, chunk), BF16),
+            pltpu.VMEM((group, 8, chunk + 128), BF16),
             pltpu.VMEM((group, 8, chunk), F32),
             pltpu.VMEM((group, 8, waves), F32),
             pltpu.VMEM((group, 128), I32),
@@ -323,18 +331,21 @@
     )(place, codes, local, across, *beyond)
     other = lax.ppermute(to_other, "bulk", side_outer)
     sibling = lax.ppermute(to_sibling, "bulk", side_inner)
-    partial = pl.pallas_call(
+    partial, mine = pl.pallas_call(
         receive_kernel,
-        out_shape=jax.ShapeDtypeStruct((2, waves, unknowns), F32),
-        in_specs=[VMEM] * 4,
-        out_specs=VMEM,
+        out_shape=(
+            jax.ShapeDtypeStruct((2, waves, unknowns), F32),
+            jax.ShapeDtypeStruct(local.shape, BF16),
+        ),
+        in_specs=[SMEM] * 2 + [VMEM] * 7,
+        out_specs=(VMEM, VMEM),
         name="receive",
         **params(8 * waves * unknowns * angles, 3 << 20),
-    )(incoming, receive[0], local, near_blocks)
+    )(place, near_list, incoming, receive[0], local, near_blocks, across, *beyond)
     return pl.pallas_call(
         near_kernel,
         out_shape=jax.ShapeDtypeStruct((1, *local.shape), BF16),
-        in_specs=[SMEM] * 2 + [VMEM] * 7,
+        in_specs=[SMEM] * 2 + [VMEM] * 5,
         out_specs=HBM,
         scratch_shapes=[
             pltpu.VMEM(local.shape, BF16),
@@ -343,7 +354,7 @@
         ],
         name="near",
         **params(8 * waves * unknowns * unknowns, 5 << 20),
-    )(place, near_list, partial, across, *beyond, other, sibling, near_blocks)
+    )(place, near_list, partial, mine, other, sibling, near_blocks)
 
 
 def solution(mesh):

time: 68.3 us -> 67.6 us (0.990)
  waiting for transfers between devices: 15.2 us -> 13.3 us
    ppermute x1, waiting for transfers between devices: 4.83 us -> 2.91 us  [per_device(): other = lax.ppermute(to_other, 'bulk', side_outer)]
    pallas_call x1, Pallas kernels: 1.33 us -> 2.6 us  [per_device(): pl.pallas_call(receive_kernel, out_shape=(jax.ShapeDtypeStruct((2, waves,...]
  transfers between devices with their start and end apart: 8 -> 8, of which waited for: 3 -> 3; matrix products, arithmetic and copies ran while one was open for 0% -> 0% of each run, Pallas kernels for 16% -> 18%
where the time goes in v4:
time: 67.6 us; the launch traced here: 67 us
  starting transfers between devices  34.3 us (51%)
  Pallas kernels  14.6 us (22%)
  waiting for transfers between devices  13.3 us (20%)
  local copies, waits for them, and re-layouts  3.35 us (5%)
  between operations  1.42 us (2%)
    all_to_all x1, starting transfers between devices, per_device(): spread = lax.all_to_all(payload, 'bulk', 0, 0, tiled=True)  9.32 us
    ppermute x1, starting transfers between devices, per_device(): lax.ppermute(relayed, axes, onward)  6.24 us
    all_to_all x1, waiting for transfers between devices, per_device(): incoming = lax.all_to_all(translated, 'bulk', 0, 0, tiled=True)  5.82 us
    all_to_all x1, starting transfers between devices, per_device(): incoming = lax.all_to_all(translated, 'bulk', 0, 0, tiled=True)  5.44 us
    all_to_all x1, waiting for transfers between devices, per_device(): spread = lax.all_to_all(payload, 'bulk', 0, 0, tiled=True)  4.58 us
    ppermute x1, starting transfers between devices, per_device(): relayed = gate(lax.ppermute(local, axes, aside), 3000000000)  4.51 us
    pallas_call x1, Pallas kernels, per_device(): pl.pallas_call(translate_kernel, out_shape=(jax.ShapeDtypeStruct((group,...  4.29 us
    unnamed x14, local copies, waits for them, and re-layouts  3.35 us
  transfers between devices with their start and end apart: 8, of which 3 were waited for; matrix products, arithmetic and copies ran while one was open for 0% of the time, Pallas kernels for 18%

profile of v4, /device:TPU:137, one launch (start us, length us, event | category | flops | bytes accessed | tf_op | source)
XLA Modules:
  0.0 67.0 jit_solution(15314370063724521356)
XLA Ops:
  0.0 0.0 copy-start.1
  0.0 4.5 %collective-permute-start.2 = (bf16[2,256,512]{2,1,0:T(8,128)(2,1)}, bf16[2,256,512]{2,1,0:T(8,128)(2,1)S(1)}, u32[]{:S(2)}, u32[]{:S(2)}) collective-permute-start(bf16[2,256,512]{2,1,0:T(8,128)(2,1)} %bitcast.6), channel_id=1, source_target_pairs={{97,1},{99,3},{101,5},{103,7},{105,9},{107,11},{109,13},{111,15},{... | collective-permute-start | bytes 1572872 | tf_op jit(solution)/shard_map/ppermute | solution.py:300
  5.8 2.7 %radiate.1 = bf16[32,8,896]{2,1,0:T(8,128)(2,1)} custom-call(s32[1,6]{1,0:T(1,128)} %far_list_at.1, s32[1]{0:T(128)S(6)} %copy.13.far_count_at, s32[1,1]{1,0:T(1,128)S(6)} %copy.12.near_list_at.near_list, s32[512]{0:T(512)} %owner_at.1, bf16[2,256,512]{2,1,0:T(8,128)(2,1)} %bitcast.7, bf16[2,512,384]{2,1,0:T(8,128)(2,1)} %bitcast.13, f32[6,2,384]{2,1,0:T(2,128)} %bitcast.14), custom_call_target="tpu_custom_call" | custom-call | flops 402653184 | bytes 2097152 | tf_op jit(solution)/shard_map/radiate/pallas_call | solution.py:268
  8.5 9.3 %all-to-all-start = ((bf16[32,8,896]{2,1,0:T(8,128)(2,1)}), bf16[32,8,896]{2,1,0:T(8,128)(2,1)}, u32[]{:S(2)}, u32[]{:S(2)}) async-start(bf16[32,8,896]{2,1,0:T(8,128)(2,1)} %radiate.1), calls=%async_computation | async-start | bytes 917504 | tf_op jit(solution)/shard_map/all_to_all | solution.py:289
  17.9 0.0 copy-done.1
  17.9 1.9 %collective-permute-start = (bf16[2,256,512]{2,1,0:T(8,128)(2,1)S(1)}, bf16[2,256,512]{2,1,0:T(8,128)(2,1)S(1)}, u32[]{:S(2)}, u32[]{:S(2)}) collective-permute-start(bf16[2,256,512]{2,1,0:T(8,128)(2,1)S(1)} %bitcast.8), channel_id=1, source_target_pairs={{0,32},{32,0},{64,96},{96,64},{128,160},{160,128},{192,224},{224,1... | collective-permute-start | bytes 1572872 | tf_op jit(solution)/shard_map/ppermute | solution.py:302
  19.8 1.5 %collective-permute-start.1 = (bf16[2,256,512]{2,1,0:T(8,128)(2,1)S(1)}, bf16[2,256,512]{2,1,0:T(8,128)(2,1)}, u32[]{:S(2)}, u32[]{:S(2)}) collective-permute-start(bf16[2,256,512]{2,1,0:T(8,128)(2,1)S(1)} %bitcast.9), channel_id=1, source_target_pairs={{32,64},{33,65},{34,66},{35,67},{36,68},{37,69},{38,70},{39,71},{4... | collective-permute-start | bytes 1572872 | tf_op jit(solution)/shard_map/ppermute | solution.py:301
  21.3 0.0 collective-permute-done.2.arrived
  21.3 0.0 copy-start.6
  21.3 0.8 %copy-done.6 = bf16[2,256,512]{2,1,0:T(8,128)(2,1)} copy-done((bf16[2,256,512]{2,1,0:T(8,128)(2,1)}, bf16[2,256,512]{2,1,0:T(8,128)(2,1)S(1)}, u32[]{:S(2)}) %copy-start.6) | copy-done | bytes 524312
  22.1 0.0 copy-start
  22.1 6.2 %collective-permute-start.3 = (bf16[2,256,512]{2,1,0:T(8,128)(2,1)}, bf16[2,256,512]{2,1,0:T(8,128)(2,1)}, u32[]{:S(2)}, u32[]{:S(2)}) collective-permute-start(bf16[2,256,512]{2,1,0:T(8,128)(2,1)} %copy-done.6), channel_id=1, source_target_pairs={{1,129},{3,131},{5,133},{7,135},{9,137},{11,139},{13,141},{15,143}... | collective-permute-start | bytes 1572872 | tf_op jit(solution)/shard_map/ppermute | solution.py:301
  28.3 4.6 %all-to-all-done.chunks_at = bf16[32,8,896]{2,1,0:T(8,128)(2,1)} async-done(((bf16[32,8,896]{2,1,0:T(8,128)(2,1)}), bf16[32,8,896]{2,1,0:T(8,128)(2,1)}, u32[]{:S(2)}, u32[]{:S(2)}) %all-to-all-start) | async-done | bytes 458784 | tf_op jit(solution)/shard_map/all_to_all | solution.py:289
  32.9 4.3 %translate.1 = (bf16[32,8,768]{2,1,0:T(8,128)(2,1)S(1)}, s32[32,128]{1,0:T(8,128)S(1)}) custom-call(bf16[32,8,896]{2,1,0:T(8,128)(2,1)} %all-to-all-done.chunks_at), custom_call_target="tpu_custom_call" | custom-call | flops 41943040 | bytes 1048576 | tf_op jit(solution)/shard_map/translate/pallas_call | solution.py:303
  37.2 0.0 copy-start.3
  37.2 0.7 %copy-done.3 = bf16[32,8,768]{2,1,0:T(8,128)(2,1)} copy-done((bf16[32,8,768]{2,1,0:T(8,128)(2,1)}, bf16[32,8,768]{2,1,0:T(8,128)(2,1)S(1)}, u32[]{:S(2)}) %copy-start.3) | copy-done | bytes 393240
  38.0 5.4 %all-to-all-start.1 = ((bf16[32,8,768]{2,1,0:T(8,128)(2,1)}), bf16[32,8,768]{2,1,0:T(8,128)(2,1)S(1)}, u32[]{:S(2)}, u32[]{:S(2)}) async-start(bf16[32,8,768]{2,1,0:T(8,128)(2,1)} %copy-done.3), calls=%async_computation.1 | async-start | bytes 786432 | tf_op jit(solution)/shard_map/all_to_all | solution.py:323
  43.4 0.1 pad_add_fusion.place
  43.5 0.0 copy-start.4
  43.5 0.0 collective-permute-done.across
  43.5 0.0 collective-permute-done.1.beyond
  43.5 0.0 collective-permute-done.3.relayed
  43.5 2.3 %select.1 = (bf16[2,256,512]{2,1,0:T(8,128)(2,1)}, bf16[2,256,512]{2,1,0:T(8,128)(2,1)}) custom-call(s32[2]{0:T(128)S(1)} %pad_add_fusion.place, s32[32,128]{1,0:T(8,128)S(1)} %get-tuple-element.14.codes, bf16[2,256,512]{2,1,0:T(8,128)(2,1)S(1)} %bitcast.10, bf16[2,256,512]{2,1,0:T(8,128)(2,1)S(1)} %collective-permute-done.across, ...), custom_call_target="tpu_custom_call" | custom-call | bytes 2097152 | tf_op jit(solution)/shard_map/select/pallas_call | solution.py:324
  45.8 3.3 %collective-permute-start.4 = (bf16[2,256,512]{2,1,0:T(8,128)(2,1)}, bf16[2,256,512]{2,1,0:T(8,128)(2,1)}, u32[]{:S(2)}, u32[]{:S(2)}) collective-permute-start(bf16[2,256,512]{2,1,0:T(8,128)(2,1)} %get-tuple-element.15), channel_id=1, source_target_pairs={{1,2},{2,1},{3,4},{4,3},{5,6},{6,5},{7,8},{8,7},{9,10},{10,9},{11,... | collective-permute-start | bytes 1572872 | tf_op jit(solution)/shard_map/ppermute | solution.py:332
  49.2 0.0 copy-done.4
  49.2 2.0 %collective-permute-start.5 = (bf16[2,256,512]{2,1,0:T(8,128)(2,1)}, bf16[2,256,512]{2,1,0:T(8,128)(2,1)}, u32[]{:S(2)}, u32[]{:S(2)}) collective-permute-start(bf16[2,256,512]{2,1,0:T(8,128)(2,1)} %get-tuple-element.16), channel_id=1, source_target_pairs={{0,1},{1,0},{2,3},{3,2},{4,5},{5,4},{6,7},{7,6},{8,9},{9,8},{10,11... | collective-permute-start | bytes 1572872 | tf_op jit(solution)/shard_map/ppermute | solution.py:333
  51.2 5.8 %all-to-all-done.1.incoming = bf16[32,8,768]{2,1,0:T(8,128)(2,1)S(1)} async-done(((bf16[32,8,768]{2,1,0:T(8,128)(2,1)}), bf16[32,8,768]{2,1,0:T(8,128)(2,1)S(1)}, u32[]{:S(2)}, u32[]{:S(2)}) %all-to-all-start.1) | async-done | bytes 393248 | tf_op jit(solution)/shard_map/all_to_all | solution.py:323
  57.0 0.0 copy-done
  57.1 0.0 copy-start.2
  57.1 1.1 %copy-done.2 = bf16[1,2,384,512]{3,2,1,0:T(8,128)(2,1)S(1)} copy-done((bf16[1,2,384,512]{3,2,1,0:T(8,128)(2,1)S(1)}, bf16[1,2,384,512]{3,2,1,0:T(8,128)(2,1)}, u32[]{:S(2)}) %copy-start.2) | copy-done | bytes 786456
  58.2 0.0 copy-start.5
  58.2 0.7 copy-done.5
  58.9 2.6 %receive.1 = (f32[2,256,512]{2,1,0:T(8,128)S(1)}, bf16[2,256,512]{2,1,0:T(8,128)(2,1)S(1)}) custom-call(s32[2]{0:T(128)S(1)} %copy-done.5, s32[1,1]{1,0:T(1,128)S(6)} %copy.12.near_list_at.near_list, bf16[32,8,768]{2,1,0:T(8,128)(2,1)S(1)} %all-to-all-done.1.incoming, bf16[2,384,512]{2,1,0:T(8,128)(2,1)S(1)} %bitcast.12, bf16[2,256,512]{2,1,0:T(8,128)(2,1)S(1)} %bitcast.11, ...), custom_call_target="tpu_custom_call" | custom-call | flops 402653184 | bytes 3145728 | tf_op jit(solution)/shard_map/receive/pallas_call | solution.py:334
  61.5 2.9 %collective-permute-done.4.other = bf16[2,256,512]{2,1,0:T(8,128)(2,1)} collective-permute-done((bf16[2,256,512]{2,1,0:T(8,128)(2,1)}, bf16[2,256,512]{2,1,0:T(8,128)(2,1)}, u32[]{:S(2)}, u32[]{:S(2)}) %collective-permute-start.4) | collective-permute-done | bytes 524320 | tf_op jit(solution)/shard_map/ppermute | solution.py:332
  64.4 0.0 collective-permute-done.5.sibling
  64.4 2.7 %near.1 = bf16[1,2,256,512]{3,2,1,0:T(8,128)(2,1)} custom-call(s32[2]{0:T(128)S(1)} %copy-done.5, s32[1,1]{1,0:T(1,128)S(6)} %copy.12.near_list_at.near_list, f32[2,256,512]{2,1,0:T(8,128)S(1)} %get-tuple-element.12.partial, bf16[2,256,512]{2,1,0:T(8,128)(2,1)S(1)} %get-tuple-element.13.mine, bf16[2,256,512]{2,1,0:T(8,128)(2,1)} %collective-permute-done.4.other, ...), custom_call_target="tpu_custom_call" | custom-call | flops 536870912 | bytes 5242880 | tf_op jit(solution)/shard_map/near/pallas_call | solution.py:345
  (1 shorter events, 0.0 us)
Async XLA Ops:
  0.0 17.9 %copy-start.1 = (bf16[1,2,256,512]{3,2,1,0:T(8,128)(2,1)S(1)}, bf16[1,2,256,512]{3,2,1,0:T(8,128)(2,1)}, u32[]{:S(2)}) copy-start(bf16[1,2,256,512]{3,2,1,0:T(8,128)(2,1)} %param.9) | copy-start | bytes 1572868
  0.0 21.3 %collective-permute-start.2 = (bf16[2,256,512]{2,1,0:T(8,128)(2,1)}, bf16[2,256,512]{2,1,0:T(8,128)(2,1)S(1)}, u32[]{:S(2)}, u32[]{:S(2)}) collective-permute-start(bf16[2,256,512]{2,1,0:T(8,128)(2,1)} %bitcast.6), channel_id=1, source_target_pairs={{97,1},{99,3},{101,5},{103,7},{105,9},{107,11},{109,13},{111,15},{... | collective-permute-start | bytes 1572872 | tf_op jit(solution)/shard_map/ppermute | solution.py:300
  8.5 24.4 %all-to-all-start = ((bf16[32,8,896]{2,1,0:T(8,128)(2,1)}), bf16[32,8,896]{2,1,0:T(8,128)(2,1)}, u32[]{:S(2)}, u32[]{:S(2)}) async-start(bf16[32,8,896]{2,1,0:T(8,128)(2,1)} %radiate.1), calls=%async_computation | async-start | bytes 917504 | tf_op jit(solution)/shard_map/all_to_all | solution.py:289
  17.9 25.6 %collective-permute-start = (bf16[2,256,512]{2,1,0:T(8,128)(2,1)S(1)}, bf16[2,256,512]{2,1,0:T(8,128)(2,1)S(1)}, u32[]{:S(2)}, u32[]{:S(2)}) collective-permute-start(bf16[2,256,512]{2,1,0:T(8,128)(2,1)S(1)} %bitcast.8), channel_id=1, source_target_pairs={{0,32},{32,0},{64,96},{96,64},{128,160},{160,128},{192,224},{224,1... | collective-permute-start | bytes 1572872 | tf_op jit(solution)/shard_map/ppermute | solution.py:302
  19.8 23.7 %collective-permute-start.1 = (bf16[2,256,512]{2,1,0:T(8,128)(2,1)S(1)}, bf16[2,256,512]{2,1,0:T(8,128)(2,1)}, u32[]{:S(2)}, u32[]{:S(2)}) collective-permute-start(bf16[2,256,512]{2,1,0:T(8,128)(2,1)S(1)} %bitcast.9), channel_id=1, source_target_pairs={{32,64},{33,65},{34,66},{35,67},{36,68},{37,69},{38,70},{39,71},{4... | collective-permute-start | bytes 1572872 | tf_op jit(solution)/shard_map/ppermute | solution.py:301
  21.3 0.8 %copy-start.6 = (bf16[2,256,512]{2,1,0:T(8,128)(2,1)}, bf16[2,256,512]{2,1,0:T(8,128)(2,1)S(1)}, u32[]{:S(2)}) copy-start(bf16[2,256,512]{2,1,0:T(8,128)(2,1)S(1)} %gate.1) | copy-start | bytes 1572868
  22.1 35.0 %copy-start = (bf16[1,2,2,512,512]{4,3,2,1,0:T(8,128)(2,1)S(1)}, bf16[1,2,2,512,512]{4,3,2,1,0:T(8,128)(2,1)}, u32[]{:S(2)}) copy-start(bf16[1,2,2,512,512]{4,3,2,1,0:T(8,128)(2,1)} %blocks.3) | copy-start | bytes 6291460
  22.1 21.4 %collective-permute-start.3 = (bf16[2,256,512]{2,1,0:T(8,128)(2,1)}, bf16[2,256,512]{2,1,0:T(8,128)(2,1)}, u32[]{:S(2)}, u32[]{:S(2)}) collective-permute-start(bf16[2,256,512]{2,1,0:T(8,128)(2,1)} %copy-done.6), channel_id=1, source_target_pairs={{1,129},{3,131},{5,133},{7,135},{9,137},{11,139},{13,141},{15,143}... | collective-permute-start | bytes 1572872 | tf_op jit(solution)/shard_map/ppermute | solution.py:301
  37.2 0.8 %copy-start.3 = (bf16[32,8,768]{2,1,0:T(8,128)(2,1)}, bf16[32,8,768]{2,1,0:T(8,128)(2,1)S(1)}, u32[]{:S(2)}) copy-start(bf16[32,8,768]{2,1,0:T(8,128)(2,1)S(1)} %get-tuple-element.11) | copy-start | bytes 1179652
  38.0 19.1 %all-to-all-start.1 = ((bf16[32,8,768]{2,1,0:T(8,128)(2,1)}), bf16[32,8,768]{2,1,0:T(8,128)(2,1)S(1)}, u32[]{:S(2)}, u32[]{:S(2)}) async-start(bf16[32,8,768]{2,1,0:T(8,128)(2,1)} %copy-done.3), calls=%async_computation.1 | async-start | bytes 786432 | tf_op jit(solution)/shard_map/all_to_all | solution.py:323
  43.5 5.7 %copy-start.4 = (s32[2]{0:T(128)}, s32[2]{0:T(128)S(1)}, u32[]{:S(2)}) copy-start(s32[2]{0:T(128)S(1)} %pad_add_fusion.place) | copy-start | bytes 28
  45.8 18.5 %collective-permute-start.4 = (bf16[2,256,512]{2,1,0:T(8,128)(2,1)}, bf16[2,256,512]{2,1,0:T(8,128)(2,1)}, u32[]{:S(2)}, u32[]{:S(2)}) collective-permute-start(bf16[2,256,512]{2,1,0:T(8,128)(2,1)} %get-tuple-element.15), channel_id=1, source_target_pairs={{1,2},{2,1},{3,4},{4,3},{5,6},{6,5},{7,8},{8,7},{9,10},{10,9},{11,... | collective-permute-start | bytes 1572872 | tf_op jit(solution)/shard_map/ppermute | solution.py:332
  49.2 15.2 %collective-permute-start.5 = (bf16[2,256,512]{2,1,0:T(8,128)(2,1)}, bf16[2,256,512]{2,1,0:T(8,128)(2,1)}, u32[]{:S(2)}, u32[]{:S(2)}) collective-permute-start(bf16[2,256,512]{2,1,0:T(8,128)(2,1)} %get-tuple-element.16), channel_id=1, source_target_pairs={{0,1},{1,0},{2,3},{3,2},{4,5},{5,4},{6,7},{7,6},{8,9},{9,8},{10,11... | collective-permute-start | bytes 1572872 | tf_op jit(solution)/shard_map/ppermute | solution.py:333
  57.1 1.1 %copy-start.2 = (bf16[1,2,384,512]{3,2,1,0:T(8,128)(2,1)S(1)}, bf16[1,2,384,512]{3,2,1,0:T(8,128)(2,1)}, u32[]{:S(2)}) copy-start(bf16[1,2,384,512]{3,2,1,0:T(8,128)(2,1)} %param.13) | copy-start | bytes 2359300
  58.2 0.7 copy-start.5

commit v5 on v4

--- a/solution.py
+++ b/solution.py
@@ -73,19 +73,22 @@
         source = lax.rem(owner[far_list[0, k]], group).astype(F32)
         table[SOURCE + k : SOURCE + k + 1, :] = jnp.full((1, angles), source, F32)
     table[CODE : CODE + 1, :] = jnp.full((1, angles), near_list[0, 0].astype(F32), F32)
-    for copy in copies[len(small) :]:
-        copy.wait()
+    tiles = angles // 8
+    factors = table[...].T.reshape(tiles, 8, table.shape[0])
     waves = currents.shape[1]
 
     def turned(part, side):
         return lax.dot_general(radiate[part], currents[side], (((0,), (1,)), ((), ())), preferred_element_type=F32)
 
-    real = turned(0, 0) - turned(1, 1)
-    imag = turned(1, 0) + turned(0, 1)
-    tiles = angles // 8
-    real = real.reshape(tiles, 8, waves)
-    imag = imag.reshape(tiles, 8, waves)
-    factors = table[...].T.reshape(tiles, 8, table.shape[0])
+    re_waves, im_waves, re_map, im_map = copies[len(small) :]
+    re_waves.wait()
+    re_map.wait()
+    real = turned(0, 0)
+    im_waves.wait()
+    imag = turned(0, 1)
+    im_map.wait()
+    real = (real - turned(1, 1)).reshape(tiles, 8, waves)
+    imag = (imag + turned(1, 0)).reshape(tiles, 8, waves)
     lane = lax.broadcasted_iota(I32, factors.shape[1:], 1)
     in_mixed = (lane >= MIXED) & (lane < SOURCE)
     def result(step):

time: 67.6 us -> 67.9 us (level)
  no operation moved by 1% of the time
where the time goes in v5:
time: 67.9 us; the launch traced here: 67.3 us
  starting transfers between devices  34.3 us (51%)
  Pallas kernels  14.9 us (22%)
  waiting for transfers between devices  13.3 us (20%)
  local copies, waits for them, and re-layouts  3.35 us (5%)
  between operations  1.42 us (2%)
    all_to_all x1, starting transfers between devices, per_device(): spread = lax.all_to_all(payload, 'bulk', 0, 0, tiled=True)  9.34 us
    ppermute x1, starting transfers between devices, per_device(): lax.ppermute(relayed, axes, onward)  6.22 us
    all_to_all x1, waiting for transfers between devices, per_device(): incoming = lax.all_to_all(translated, 'bulk', 0, 0, tiled=True)  5.82 us
    all_to_all x1, starting transfers between devices, per_device(): incoming = lax.all_to_all(translated, 'bulk', 0, 0, tiled=True)  5.44 us
    all_to_all x1, waiting for transfers between devices, per_device(): spread = lax.all_to_all(payload, 'bulk', 0, 0, tiled=True)  4.59 us
    ppermute x1, starting transfers between devices, per_device(): relayed = gate(lax.ppermute(local, axes, aside), 3000000000)  4.51 us
    pallas_call x1, Pallas kernels, per_device(): pl.pallas_call(translate_kernel, out_shape=(jax.ShapeDtypeStruct((group,...  4.27 us
    unnamed x14, local copies, waits for them, and re-layouts  3.35 us
  transfers between devices with their start and end apart: 8, of which 3 were waited for; matrix products, arithmetic and copies ran while one was open for 0% of the time, Pallas kernels for 18%

profile of v5, /device:TPU:137, one launch (start us, length us, event | category | flops | bytes accessed | tf_op | source)
XLA Modules:
  0.0 67.3 jit_solution(8778930742131220665)
XLA Ops:
  0.0 0.0 copy-start.1
  0.0 4.5 %collective-permute-start.2 = (bf16[2,256,512]{2,1,0:T(8,128)(2,1)}, bf16[2,256,512]{2,1,0:T(8,128)(2,1)S(1)}, u32[]{:S(2)}, u32[]{:S(2)}) collective-permute-start(bf16[2,256,512]{2,1,0:T(8,128)(2,1)} %bitcast.6), channel_id=1, source_target_pairs={{97,1},{99,3},{101,5},{103,7},{105,9},{107,11},{109,13},{111,15},{... | collective-permute-start | bytes 1572872 | tf_op jit(solution)/shard_map/ppermute | solution.py:303
  5.8 3.0 %radiate.1 = bf16[32,8,896]{2,1,0:T(8,128)(2,1)} custom-call(s32[1,6]{1,0:T(1,128)} %far_list_at.1, s32[1]{0:T(128)S(6)} %copy.13.far_count_at, s32[1,1]{1,0:T(1,128)S(6)} %copy.12.near_list_at.near_list, s32[512]{0:T(512)} %owner_at.1, bf16[2,256,512]{2,1,0:T(8,128)(2,1)} %bitcast.7, bf16[2,512,384]{2,1,0:T(8,128)(2,1)} %bitcast.13, f32[6,2,384]{2,1,0:T(2,128)} %bitcast.14), custom_call_target="tpu_custom_call" | custom-call | flops 402653184 | bytes 2097152 | tf_op jit(solution)/shard_map/radiate/pallas_call | solution.py:271
  8.9 9.3 %all-to-all-start = ((bf16[32,8,896]{2,1,0:T(8,128)(2,1)}), bf16[32,8,896]{2,1,0:T(8,128)(2,1)}, u32[]{:S(2)}, u32[]{:S(2)}) async-start(bf16[32,8,896]{2,1,0:T(8,128)(2,1)} %radiate.1), calls=%async_computation | async-start | bytes 917504 | tf_op jit(solution)/shard_map/all_to_all | solution.py:292
  18.2 0.0 copy-done.1
  18.2 1.9 %collective-permute-start = (bf16[2,256,512]{2,1,0:T(8,128)(2,1)S(1)}, bf16[2,256,512]{2,1,0:T(8,128)(2,1)S(1)}, u32[]{:S(2)}, u32[]{:S(2)}) collective-permute-start(bf16[2,256,512]{2,1,0:T(8,128)(2,1)S(1)} %bitcast.8), channel_id=1, source_target_pairs={{0,32},{32,0},{64,96},{96,64},{128,160},{160,128},{192,224},{224,1... | collective-permute-start | bytes 1572872 | tf_op jit(solution)/shard_map/ppermute | solution.py:305
  20.1 1.5 %collective-permute-start.1 = (bf16[2,256,512]{2,1,0:T(8,128)(2,1)S(1)}, bf16[2,256,512]{2,1,0:T(8,128)(2,1)}, u32[]{:S(2)}, u32[]{:S(2)}) collective-permute-start(bf16[2,256,512]{2,1,0:T(8,128)(2,1)S(1)} %bitcast.9), channel_id=1, source_target_pairs={{32,64},{33,65},{34,66},{35,67},{36,68},{37,69},{38,70},{39,71},{4... | collective-permute-start | bytes 1572872 | tf_op jit(solution)/shard_map/ppermute | solution.py:304
  21.6 0.0 collective-permute-done.2.arrived
  21.6 0.0 copy-start.6
  21.6 0.8 %copy-done.6 = bf16[2,256,512]{2,1,0:T(8,128)(2,1)} copy-done((bf16[2,256,512]{2,1,0:T(8,128)(2,1)}, bf16[2,256,512]{2,1,0:T(8,128)(2,1)S(1)}, u32[]{:S(2)}) %copy-start.6) | copy-done | bytes 524312
  22.4 0.0 copy-start
  22.4 6.2 %collective-permute-start.3 = (bf16[2,256,512]{2,1,0:T(8,128)(2,1)}, bf16[2,256,512]{2,1,0:T(8,128)(2,1)}, u32[]{:S(2)}, u32[]{:S(2)}) collective-permute-start(bf16[2,256,512]{2,1,0:T(8,128)(2,1)} %copy-done.6), channel_id=1, source_target_pairs={{1,129},{3,131},{5,133},{7,135},{9,137},{11,139},{13,141},{15,143}... | collective-permute-start | bytes 1572872 | tf_op jit(solution)/shard_map/ppermute | solution.py:304
  28.6 4.6 %all-to-all-done.chunks_at = bf16[32,8,896]{2,1,0:T(8,128)(2,1)} async-done(((bf16[32,8,896]{2,1,0:T(8,128)(2,1)}), bf16[32,8,896]{2,1,0:T(8,128)(2,1)}, u32[]{:S(2)}, u32[]{:S(2)}) %all-to-all-start) | async-done | bytes 458784 | tf_op jit(solution)/shard_map/all_to_all | solution.py:292
  33.2 4.3 %translate.1 = (bf16[32,8,768]{2,1,0:T(8,128)(2,1)S(1)}, s32[32,128]{1,0:T(8,128)S(1)}) custom-call(bf16[32,8,896]{2,1,0:T(8,128)(2,1)} %all-to-all-done.chunks_at), custom_call_target="tpu_custom_call" | custom-call | flops 41943040 | bytes 1048576 | tf_op jit(solution)/shard_map/translate/pallas_call | solution.py:306
  37.5 0.0 copy-start.3
  37.5 0.7 %copy-done.3 = bf16[32,8,768]{2,1,0:T(8,128)(2,1)} copy-done((bf16[32,8,768]{2,1,0:T(8,128)(2,1)}, bf16[32,8,768]{2,1,0:T(8,128)(2,1)S(1)}, u32[]{:S(2)}) %copy-start.3) | copy-done | bytes 393240
  38.3 5.4 %all-to-all-start.1 = ((bf16[32,8,768]{2,1,0:T(8,128)(2,1)}), bf16[32,8,768]{2,1,0:T(8,128)(2,1)S(1)}, u32[]{:S(2)}, u32[]{:S(2)}) async-start(bf16[32,8,768]{2,1,0:T(8,128)(2,1)} %copy-done.3), calls=%async_computation.1 | async-start | bytes 786432 | tf_op jit(solution)/shard_map/all_to_all | solution.py:326
  43.7 0.1 pad_add_fusion.place
  43.8 0.0 copy-start.4
  43.8 0.0 collective-permute-done.across
  43.8 0.0 collective-permute-done.1.beyond
  43.8 0.0 collective-permute-done.3.relayed
  43.8 2.3 %select.1 = (bf16[2,256,512]{2,1,0:T(8,128)(2,1)}, bf16[2,256,512]{2,1,0:T(8,128)(2,1)}) custom-call(s32[2]{0:T(128)S(1)} %pad_add_fusion.place, s32[32,128]{1,0:T(8,128)S(1)} %get-tuple-element.14.codes, bf16[2,256,512]{2,1,0:T(8,128)(2,1)S(1)} %bitcast.10, bf16[2,256,512]{2,1,0:T(8,128)(2,1)S(1)} %collective-permute-done.across, ...), custom_call_target="tpu_custom_call" | custom-call | bytes 2097152 | tf_op jit(solution)/shard_map/select/pallas_call | solution.py:327
  46.1 3.3 %collective-permute-start.4 = (bf16[2,256,512]{2,1,0:T(8,128)(2,1)}, bf16[2,256,512]{2,1,0:T(8,128)(2,1)}, u32[]{:S(2)}, u32[]{:S(2)}) collective-permute-start(bf16[2,256,512]{2,1,0:T(8,128)(2,1)} %get-tuple-element.15), channel_id=1, source_target_pairs={{1,2},{2,1},{3,4},{4,3},{5,6},{6,5},{7,8},{8,7},{9,10},{10,9},{11,... | collective-permute-start | bytes 1572872 | tf_op jit(solution)/shard_map/ppermute | solution.py:335
  49.5 0.0 copy-done.4
  49.5 2.0 %collective-permute-start.5 = (bf16[2,256,512]{2,1,0:T(8,128)(2,1)}, bf16[2,256,512]{2,1,0:T(8,128)(2,1)}, u32[]{:S(2)}, u32[]{:S(2)}) collective-permute-start(bf16[2,256,512]{2,1,0:T(8,128)(2,1)} %get-tuple-element.16), channel_id=1, source_target_pairs={{0,1},{1,0},{2,3},{3,2},{4,5},{5,4},{6,7},{7,6},{8,9},{9,8},{10,11... | collective-permute-start | bytes 1572872 | tf_op jit(solution)/shard_map/ppermute | solution.py:336
  51.5 5.8 %all-to-all-done.1.incoming = bf16[32,8,768]{2,1,0:T(8,128)(2,1)S(1)} async-done(((bf16[32,8,768]{2,1,0:T(8,128)(2,1)}), bf16[32,8,768]{2,1,0:T(8,128)(2,1)S(1)}, u32[]{:S(2)}, u32[]{:S(2)}) %all-to-all-start.1) | async-done | bytes 393248 | tf_op jit(solution)/shard_map/all_to_all | solution.py:326
  57.4 0.0 copy-done
  57.4 0.0 copy-start.2
  57.4 1.1 %copy-done.2 = bf16[1,2,384,512]{3,2,1,0:T(8,128)(2,1)S(1)} copy-done((bf16[1,2,384,512]{3,2,1,0:T(8,128)(2,1)S(1)}, bf16[1,2,384,512]{3,2,1,0:T(8,128)(2,1)}, u32[]{:S(2)}) %copy-start.2) | copy-done | bytes 786456
  58.5 0.0 copy-start.5
  58.5 0.7 copy-done.5
  59.2 2.6 %receive.1 = (f32[2,256,512]{2,1,0:T(8,128)S(1)}, bf16[2,256,512]{2,1,0:T(8,128)(2,1)S(1)}) custom-call(s32[2]{0:T(128)S(1)} %copy-done.5, s32[1,1]{1,0:T(1,128)S(6)} %copy.12.near_list_at.near_list, bf16[32,8,768]{2,1,0:T(8,128)(2,1)S(1)} %all-to-all-done.1.incoming, bf16[2,384,512]{2,1,0:T(8,128)(2,1)S(1)} %bitcast.12, bf16[2,256,512]{2,1,0:T(8,128)(2,1)S(1)} %bitcast.11, ...), custom_call_target="tpu_custom_call" | custom-call | flops 402653184 | bytes 3145728 | tf_op jit(solution)/shard_map/receive/pallas_call | solution.py:337
  61.8 2.9 %collective-permute-done.4.other = bf16[2,256,512]{2,1,0:T(8,128)(2,1)} collective-permute-done((bf16[2,256,512]{2,1,0:T(8,128)(2,1)}, bf16[2,256,512]{2,1,0:T(8,128)(2,1)}, u32[]{:S(2)}, u32[]{:S(2)}) %collective-permute-start.4) | collective-permute-done | bytes 524320 | tf_op jit(solution)/shard_map/ppermute | solution.py:335
  64.7 0.0 collective-permute-done.5.sibling
  64.7 2.7 %near.1 = bf16[1,2,256,512]{3,2,1,0:T(8,128)(2,1)} custom-call(s32[2]{0:T(128)S(1)} %copy-done.5, s32[1,1]{1,0:T(1,128)S(6)} %copy.12.near_list_at.near_list, f32[2,256,512]{2,1,0:T(8,128)S(1)} %get-tuple-element.12.partial, bf16[2,256,512]{2,1,0:T(8,128)(2,1)S(1)} %get-tuple-element.13.mine, bf16[2,256,512]{2,1,0:T(8,128)(2,1)} %collective-permute-done.4.other, ...), custom_call_target="tpu_custom_call" | custom-call | flops 536870912 | bytes 5242880 | tf_op jit(solution)/shard_map/near/pallas_call | solution.py:348
  (1 shorter events, 0.0 us)
Async XLA Ops:
  0.0 18.2 %copy-start.1 = (bf16[1,2,256,512]{3,2,1,0:T(8,128)(2,1)S(1)}, bf16[1,2,256,512]{3,2,1,0:T(8,128)(2,1)}, u32[]{:S(2)}) copy-start(bf16[1,2,256,512]{3,2,1,0:T(8,128)(2,1)} %param.9) | copy-start | bytes 1572868
  0.0 21.6 %collective-permute-start.2 = (bf16[2,256,512]{2,1,0:T(8,128)(2,1)}, bf16[2,256,512]{2,1,0:T(8,128)(2,1)S(1)}, u32[]{:S(2)}, u32[]{:S(2)}) collective-permute-start(bf16[2,256,512]{2,1,0:T(8,128)(2,1)} %bitcast.6), channel_id=1, source_target_pairs={{97,1},{99,3},{101,5},{103,7},{105,9},{107,11},{109,13},{111,15},{... | collective-permute-start | bytes 1572872 | tf_op jit(solution)/shard_map/ppermute | solution.py:303
  8.9 24.4 %all-to-all-start = ((bf16[32,8,896]{2,1,0:T(8,128)(2,1)}), bf16[32,8,896]{2,1,0:T(8,128)(2,1)}, u32[]{:S(2)}, u32[]{:S(2)}) async-start(bf16[32,8,896]{2,1,0:T(8,128)(2,1)} %radiate.1), calls=%async_computation | async-start | bytes 917504 | tf_op jit(solution)/shard_map/all_to_all | solution.py:292
  18.2 25.6 %collective-permute-start = (bf16[2,256,512]{2,1,0:T(8,128)(2,1)S(1)}, bf16[2,256,512]{2,1,0:T(8,128)(2,1)S(1)}, u32[]{:S(2)}, u32[]{:S(2)}) collective-permute-start(bf16[2,256,512]{2,1,0:T(8,128)(2,1)S(1)} %bitcast.8), channel_id=1, source_target_pairs={{0,32},{32,0},{64,96},{96,64},{128,160},{160,128},{192,224},{224,1... | collective-permute-start | bytes 1572872 | tf_op jit(solution)/shard_map/ppermute | solution.py:305
  20.1 23.7 %collective-permute-start.1 = (bf16[2,256,512]{2,1,0:T(8,128)(2,1)S(1)}, bf16[2,256,512]{2,1,0:T(8,128)(2,1)}, u32[]{:S(2)}, u32[]{:S(2)}) collective-permute-start(bf16[2,256,512]{2,1,0:T(8,128)(2,1)S(1)} %bitcast.9), channel_id=1, source_target_pairs={{32,64},{33,65},{34,66},{35,67},{36,68},{37,69},{38,70},{39,71},{4... | collective-permute-start | bytes 1572872 | tf_op jit(solution)/shard_map/ppermute | solution.py:304
  21.6 0.8 %copy-start.6 = (bf16[2,256,512]{2,1,0:T(8,128)(2,1)}, bf16[2,256,512]{2,1,0:T(8,128)(2,1)S(1)}, u32[]{:S(2)}) copy-start(bf16[2,256,512]{2,1,0:T(8,128)(2,1)S(1)} %gate.1) | copy-start | bytes 1572868
  22.4 34.9 %copy-start = (bf16[1,2,2,512,512]{4,3,2,1,0:T(8,128)(2,1)S(1)}, bf16[1,2,2,512,512]{4,3,2,1,0:T(8,128)(2,1)}, u32[]{:S(2)}) copy-start(bf16[1,2,2,512,512]{4,3,2,1,0:T(8,128)(2,1)} %blocks.3) | copy-start | bytes 6291460
  22.4 21.4 %collective-permute-start.3 = (bf16[2,256,512]{2,1,0:T(8,128)(2,1)}, bf16[2,256,512]{2,1,0:T(8,128)(2,1)}, u32[]{:S(2)}, u32[]{:S(2)}) collective-permute-start(bf16[2,256,512]{2,1,0:T(8,128)(2,1)} %copy-done.6), channel_id=1, source_target_pairs={{1,129},{3,131},{5,133},{7,135},{9,137},{11,139},{13,141},{15,143}... | collective-permute-start | bytes 1572872 | tf_op jit(solution)/shard_map/ppermute | solution.py:304
  37.5 0.8 %copy-start.3 = (bf16[32,8,768]{2,1,0:T(8,128)(2,1)}, bf16[32,8,768]{2,1,0:T(8,128)(2,1)S(1)}, u32[]{:S(2)}) copy-start(bf16[32,8,768]{2,1,0:T(8,128)(2,1)S(1)} %get-tuple-element.11) | copy-start | bytes 1179652
  38.3 19.1 %all-to-all-start.1 = ((bf16[32,8,768]{2,1,0:T(8,128)(2,1)}), bf16[32,8,768]{2,1,0:T(8,128)(2,1)S(1)}, u32[]{:S(2)}, u32[]{:S(2)}) async-start(bf16[32,8,768]{2,1,0:T(8,128)(2,1)} %copy-done.3), calls=%async_computation.1 | async-start | bytes 786432 | tf_op jit(solution)/shard_map/all_to_all | solution.py:326
  43.8 5.7 %copy-start.4 = (s32[2]{0:T(128)}, s32[2]{0:T(128)S(1)}, u32[]{:S(2)}) copy-start(s32[2]{0:T(128)S(1)} %pad_add_fusion.place) | copy-start | bytes 28
  46.1 18.5 %collective-permute-start.4 = (bf16[2,256,512]{2,1,0:T(8,128)(2,1)}, bf16[2,256,512]{2,1,0:T(8,128)(2,1)}, u32[]{:S(2)}, u32[]{:S(2)}) collective-permute-start(bf16[2,256,512]{2,1,0:T(8,128)(2,1)} %get-tuple-element.15), channel_id=1, source_target_pairs={{1,2},{2,1},{3,4},{4,3},{5,6},{6,5},{7,8},{8,7},{9,10},{10,9},{11,... | collective-permute-start | bytes 1572872 | tf_op jit(solution)/shard_map/ppermute | solution.py:335
  49.5 15.2 %collective-permute-start.5 = (bf16[2,256,512]{2,1,0:T(8,128)(2,1)}, bf16[2,256,512]{2,1,0:T(8,128)(2,1)}, u32[]{:S(2)}, u32[]{:S(2)}) collective-permute-start(bf16[2,256,512]{2,1,0:T(8,128)(2,1)} %get-tuple-element.16), channel_id=1, source_target_pairs={{0,1},{1,0},{2,3},{3,2},{4,5},{5,4},{6,7},{7,6},{8,9},{9,8},{10,11... | collective-permute-start | bytes 1572872 | tf_op jit(solution)/shard_map/ppermute | solution.py:336
  57.4 1.1 %copy-start.2 = (bf16[1,2,384,512]{3,2,1,0:T(8,128)(2,1)S(1)}, bf16[1,2,384,512]{3,2,1,0:T(8,128)(2,1)}, u32[]{:S(2)}) copy-start(bf16[1,2,384,512]{3,2,1,0:T(8,128)(2,1)} %param.13) | copy-start | bytes 2359300
  58.5 0.7 copy-start.5
